TPU v7x, 32 devices: a whole 2x2x4 slice. The times are simulated.
32 devices in a mesh: dp: 16 (over z, y, core), tensor: 2 (over x).
Axes of the slice: x: 2, y: 2, z: 4, core: 2. Of those that a mesh axis runs over, the one named last changes fastest.
Arguments:
- tokens: bfloat16 [65536, 1024], P(('dp', 'tensor')), may hold values from -6 to 6
- lengths: int32 [16, 8], P('dp'), may hold values from 1 to 512, as said below
- cotangent: bfloat16 [65536, 1024], P(('dp', 'tensor')), may hold values from -6 to 6
- query_weight: bfloat16 [1024, 1024], P(None, 'tensor'), may hold values from -0.1875 to 0.1875
- query_bias: bfloat16 [1024], P('tensor'), may hold values from -3 to 3
- key_weight: bfloat16 [1024, 1024], P(None, 'tensor'), may hold values from -0.1875 to 0.1875
- value_weight: bfloat16 [1024, 1024], P(None, 'tensor'), may hold values from -0.1875 to 0.1875
- value_bias: bfloat16 [1024], P('tensor'), may hold values from -3 to 3
- out_weight: bfloat16 [1024, 1024], P('tensor'), may hold values from -0.75 to 0.75
- out_bias: bfloat16 [1024], replicated, may hold values from -3 to 3
- first_gain: float32 [1024], replicated, may hold values from 0.1 to 1.9
- first_shift: float32 [1024], replicated, may hold values from -3 to 3
- up_weight: bfloat16 [1024, 4096], P(None, 'tensor'), may hold values from -0.1875 to 0.1875
- up_bias: bfloat16 [4096], P('tensor'), may hold values from -3 to 3
- down_weight: bfloat16 [4096, 1024], P('tensor'), may hold values from -0.09375 to 0.09375
- down_bias: bfloat16 [1024], replicated, may hold values from -3 to 3
- second_gain: float32 [1024], replicated, may hold values from 0.1 to 1.9
- second_shift: float32 [1024], replicated, may hold values from -3 to 3
Outputs:
- layer_out: float32 [65536, 1024], P(('dp', 'tensor'))
- grad_tokens: float32 [65536, 1024], P(('dp', 'tensor'))
- wgrad_query: float32 [1024, 1024], P(None, 'tensor')
- bgrad_query: float32 [1024], P('tensor')
- wgrad_key: float32 [1024, 1024], P(None, 'tensor')
- wgrad_value: float32 [1024, 1024], P(None, 'tensor')
- bgrad_value: float32 [1024], P('tensor')
- wgrad_out: float32 [1024, 1024], P('tensor')
- bgrad_out: float32 [1024], replicated
- ggrad_first: float32 [1024], replicated
- sgrad_first: float32 [1024], replicated
- wgrad_up: float32 [1024, 4096], P(None, 'tensor')
- bgrad_up: float32 [4096], P('tensor')
- wgrad_down: float32 [4096, 1024], P('tensor')
- bgrad_down: float32 [1024], replicated
- ggrad_second: float32 [1024], replicated
- sgrad_second: float32 [1024], replicated
Inputs may be any that keep to these rules, and one draw needn't show every extreme that they name: `lengths`: every group has at least one slot of length 512.
All inputs are finite; a program needn't handle non-finite values.
Results may differ from a plain program's by a relative error of at most 0.02.
Values may be sent and summed in bfloat16 or wider, within the bound.
A program may use at most 320 MiB of HBM per device.

v0:
```python
from functools import partial

import jax
import jax.numpy as jnp
from jax import lax
from jax.sharding import PartitionSpec as P

HEAD_DIM = 64
SEQ_LEN = 512
SEQS = 8


epsilon = 1e-12


def normalize(summed, gain, shift):
    middle = jnp.mean(summed, axis=-1, keepdims=True)
    centred = summed - middle
    spread = jnp.mean(centred * centred, axis=-1, keepdims=True)
    return centred * lax.rsqrt(spread + epsilon) * gain + shift


def contract_rows(left, right):
    return lax.dot_general(
        left, right, (((0,), (0,)), ((), ())), preferred_element_type=jnp.float32
    )


def contract_cols(left, right):
    return lax.dot_general(
        left, right, (((1,), (1,)), ((), ())), preferred_element_type=jnp.float32
    )


def matmul(left, right):
    return jnp.dot(left, right, preferred_element_type=jnp.float32)


def block_scores(queries, key_rows, valid_keys):
    scores = jnp.einsum("qhe,khe->hqk", queries, key_rows, preferred_element_type=jnp.float32)
    scores = scores * HEAD_DIM ** (-0.5)
    return jnp.where(valid_keys[None, None, :], scores, -1e30)


def attend_block(block):
    queries, key_rows, value_rows, valid_keys = block
    scores = block_scores(queries, key_rows, valid_keys)
    row_top = jnp.max(scores, axis=-1, keepdims=True)
    raised = jnp.exp(scores - row_top)
    row_total = jnp.sum(raised, axis=-1, keepdims=True)
    attn_probs = raised / row_total
    mixed = jnp.einsum(
        "hqk,khe->qhe",
        attn_probs.astype(jnp.bfloat16),
        value_rows,
        preferred_element_type=jnp.float32,
    )
    return (mixed, (row_top + jnp.log(row_total))[..., 0])


def attend_back(block):
    queries, key_rows, value_rows, valid_keys, log_total, grad_mixed = block
    scores = block_scores(queries, key_rows, valid_keys)
    attn_probs = jnp.exp(scores - log_total[..., None])
    grad_probs = jnp.einsum(
        "qhe,khe->hqk", grad_mixed, value_rows, preferred_element_type=jnp.float32
    )
    grad_values = jnp.einsum(
        "hqk,qhe->khe",
        attn_probs.astype(jnp.bfloat16),
        grad_mixed,
        preferred_element_type=jnp.float32,
    )
    inner_sum = jnp.sum(grad_probs * attn_probs, axis=-1, keepdims=True)
    grad_scores = (attn_probs * (grad_probs - inner_sum)).astype(jnp.bfloat16)
    grad_queries = jnp.einsum(
        "hqk,khe->qhe", grad_scores, key_rows, preferred_element_type=jnp.float32
    ) * HEAD_DIM ** (-0.5)
    grad_keys = jnp.einsum(
        "hqk,qhe->khe", grad_scores, queries, preferred_element_type=jnp.float32
    ) * HEAD_DIM ** (-0.5)
    return (grad_queries, grad_keys, grad_values)


def shards(
    tokens,
    lengths,
    cotangent,
    query_weight,
    query_bias,
    key_weight,
    value_weight,
    value_bias,
    out_weight,
    out_bias,
    first_gain,
    first_shift,
    up_weight,
    up_bias,
    down_weight,
    down_bias,
    second_gain,
    second_shift,
):
    local_rows = tokens.shape[0]
    group_rows = SEQS * SEQ_LEN
    local_heads = query_weight.shape[1] // HEAD_DIM
    local_width = local_heads * HEAD_DIM
    row_index = lax.axis_index("tensor") * local_rows + jnp.arange(local_rows, dtype=jnp.int32)
    slot_match = (row_index // SEQ_LEN)[:, None] == jnp.arange(SEQS, dtype=jnp.int32)[None, :]
    row_length = jnp.sum(jnp.where(slot_match, lengths[0][None, :], 0), axis=1)
    row_live = (row_index % SEQ_LEN < row_length).astype(jnp.float32)
    valid_keys = jnp.arange(SEQ_LEN, dtype=jnp.int32)[None, :] < lengths[0][:, None]

    def split_heads(rows):
        return rows.reshape(SEQS, SEQ_LEN, local_heads, HEAD_DIM)

    gathered = lax.all_gather(tokens, "tensor", axis=0, tiled=True)
    queries = (matmul(gathered, query_weight) + query_bias.astype(jnp.float32)).astype(jnp.bfloat16)
    key_rows = matmul(gathered, key_weight).astype(jnp.bfloat16)
    value_rows = (matmul(gathered, value_weight) + value_bias.astype(jnp.float32)).astype(
        jnp.bfloat16
    )
    mixed, log_total = lax.map(
        attend_block,
        (split_heads(queries), split_heads(key_rows), split_heads(value_rows), valid_keys),
    )
    mixed = mixed.astype(jnp.bfloat16).reshape(group_rows, local_width)
    attn_sum = lax.psum_scatter(
        matmul(mixed, out_weight), "tensor", scatter_dimension=0, tiled=True
    )
    first_sum = tokens.astype(jnp.float32) + attn_sum + out_bias.astype(jnp.float32)
    hidden = normalize(first_sum, first_gain, first_shift)
    hidden_low = hidden.astype(jnp.bfloat16)
    hidden_all = lax.all_gather(hidden_low, "tensor", axis=0, tiled=True)
    inner = matmul(hidden_all, up_weight) + up_bias.astype(jnp.float32)
    active = jax.nn.gelu(inner, approximate=False).astype(jnp.bfloat16)
    branch = lax.psum_scatter(
        matmul(active, down_weight).astype(jnp.bfloat16), "tensor", scatter_dimension=0, tiled=True
    ).astype(jnp.float32)
    second_sum = hidden + branch + down_bias.astype(jnp.float32)
    layer_out = normalize(second_sum, second_gain, second_shift)
    grad_out = cotangent.astype(jnp.float32) * row_live[:, None]
    second_pull = jax.vjp(normalize, second_sum, second_gain, second_shift)[1]
    grad_second, ggrad_second, sgrad_second = second_pull(grad_out)
    bgrad_down = jnp.sum(grad_second, axis=0)
    grad_second_low = grad_second.astype(jnp.bfloat16)
    gelu_pull = jax.vjp(partial(jax.nn.gelu, approximate=False), inner)[1]
    grad_branch = lax.all_gather(grad_second_low, "tensor", axis=0, tiled=True)
    wgrad_down = contract_rows(active, grad_branch)
    grad_inner = gelu_pull(contract_cols(grad_branch, down_weight))[0]
    bgrad_up = jnp.sum(grad_inner, axis=0)
    grad_inner_low = grad_inner.astype(jnp.bfloat16)
    wgrad_up = contract_rows(hidden_all, grad_inner_low)
    back_hidden = lax.psum_scatter(
        contract_cols(grad_inner_low, up_weight).astype(jnp.bfloat16),
        "tensor",
        scatter_dimension=0,
        tiled=True,
    ).astype(jnp.float32)
    grad_hidden = grad_second + back_hidden
    first_pull = jax.vjp(normalize, first_sum, first_gain, first_shift)[1]
    grad_first, ggrad_first, sgrad_first = first_pull(grad_hidden)
    bgrad_out = jnp.sum(grad_first, axis=0)
    grad_attn = lax.all_gather(grad_first.astype(jnp.bfloat16), "tensor", axis=0, tiled=True)
    wgrad_out = contract_rows(mixed, grad_attn)
    grad_mixed = contract_cols(grad_attn, out_weight).astype(jnp.bfloat16)
    grad_queries, grad_keys, grad_values = lax.map(
        attend_back,
        (
            split_heads(queries),
            split_heads(key_rows),
            split_heads(value_rows),
            valid_keys,
            log_total,
            split_heads(grad_mixed),
        ),
    )
    grad_queries = grad_queries.reshape(group_rows, local_width)
    grad_keys = grad_keys.reshape(group_rows, local_width)
    grad_values = grad_values.reshape(group_rows, local_width)
    bgrad_query = jnp.sum(grad_queries, axis=0)
    bgrad_value = jnp.sum(grad_values, axis=0)
    queries_low = grad_queries.astype(jnp.bfloat16)
    keys_low = grad_keys.astype(jnp.bfloat16)
    values_low = grad_values.astype(jnp.bfloat16)
    wgrad_query = contract_rows(gathered, queries_low)
    wgrad_key = contract_rows(gathered, keys_low)
    wgrad_value = contract_rows(gathered, values_low)
    back_tokens = (
        contract_cols(queries_low, query_weight)
        + contract_cols(keys_low, key_weight)
        + contract_cols(values_low, value_weight)
    )
    grad_tokens = grad_first + lax.psum_scatter(
        back_tokens.astype(jnp.bfloat16), "tensor", scatter_dimension=0, tiled=True
    ).astype(jnp.float32)
    (
        wgrad_query,
        bgrad_query,
        wgrad_key,
        wgrad_value,
        bgrad_value,
        wgrad_out,
        wgrad_up,
        bgrad_up,
        wgrad_down,
    ) = (
        lax.psum(wgrad_query.astype(jnp.bfloat16), "dp").astype(jnp.float32),
        lax.psum(bgrad_query.astype(jnp.bfloat16), "dp").astype(jnp.float32),
        lax.psum(wgrad_key.astype(jnp.bfloat16), "dp").astype(jnp.float32),
        lax.psum(wgrad_value.astype(jnp.bfloat16), "dp").astype(jnp.float32),
        lax.psum(bgrad_value.astype(jnp.bfloat16), "dp").astype(jnp.float32),
        lax.psum(wgrad_out.astype(jnp.bfloat16), "dp").astype(jnp.float32),
        lax.psum(wgrad_up.astype(jnp.bfloat16), "dp").astype(jnp.float32),
        lax.psum(bgrad_up.astype(jnp.bfloat16), "dp").astype(jnp.float32),
        lax.psum(wgrad_down.astype(jnp.bfloat16), "dp").astype(jnp.float32),
    )
    bgrad_out, ggrad_first, sgrad_first, bgrad_down, ggrad_second, sgrad_second = lax.psum(
        (bgrad_out, ggrad_first, sgrad_first, bgrad_down, ggrad_second, sgrad_second),
        ("dp", "tensor"),
    )
    return (
        layer_out,
        grad_tokens,
        wgrad_query,
        bgrad_query,
        wgrad_key,
        wgrad_value,
        bgrad_value,
        wgrad_out,
        bgrad_out,
        ggrad_first,
        sgrad_first,
        wgrad_up,
        bgrad_up,
        wgrad_down,
        bgrad_down,
        ggrad_second,
        sgrad_second,
    )


def solution(mesh):
    return jax.shard_map(
        shards,
        mesh=mesh,
        in_specs=(
            P(("dp", "tensor"), None),
            P("dp", None),
            P(("dp", "tensor"), None),
            P(None, "tensor"),
            P("tensor"),
            P(None, "tensor"),
            P(None, "tensor"),
            P("tensor"),
            P("tensor", None),
            P(),
            P(),
            P(),
            P(None, "tensor"),
            P("tensor"),
            P("tensor", None),
            P(),
            P(),
            P(),
        ),
        out_specs=(
            P(("dp", "tensor"), None),
            P(("dp", "tensor"), None),
            P(None, "tensor"),
            P("tensor"),
            P(None, "tensor"),
            P(None, "tensor"),
            P("tensor"),
            P("tensor", None),
            P(),
            P(),
            P(),
            P(None, "tensor"),
            P("tensor"),
            P("tensor", None),
            P(),
            P(),
            P(),
        ),
        check_vma=False,
    )
```

profile of v0, /device:TPU:0, one launch (start us, length us, event | category | flops | bytes accessed | tf_op | source)
XLA Modules:
  0.0 1848.5 jit_solution(14070951883426965964)
XLA Ops:
  13.9 102.4 %all-gather.5.cloned.1.call-done = bf16[4096,1024]{1,0:T(8,128)(2,1)} async-done(((bf16[2048,1024]{1,0:T(8,128)(2,1)}), bf16[4096,1024]{1,0:T(8,128)(2,1)}) %all-gather.5.cloned.1.call-update) | async-done | bytes 8388624 | tf_op jit(solution)/shard_map/all_gather | solution.py:118
  116.3 9.4 add_convert_fusion.2
  125.8 11.1 reshape.204
  136.9 9.8 copy.78
  146.7 9.4 add_convert_fusion.1
  156.1 11.1 reshape.205
  167.3 9.8 copy.79
  177.1 9.4 convolution_convert_fusion.2
  186.5 11.1 reshape.206
  197.7 9.8 copy.80
  207.4 79.0 %while.28 = (s32[]{:T(128)}, bf16[8,512,8,64]{1,3,2,0:T(8,128)(2,1)}, f32[8,8,512]{2,1,0:T(8,128)}, bf16[8,512,8,64]{1,3,2,0:T(8,128)(2,1)}, pred[8,512]{1,0:T(8...) while((s32[]{:T(128)}, bf16[8,512,8,64]{1,3,2,0:T(8,128)(2,1)}, ...), condition=%wide.region_3.4_spmd.clone, body=%wide.region_0.3_spmd.sunk.clone | while | flops 562032640 | bytes 27923536 | solution.py:124
  295.4 8.1 fusion.94
  304.2 188.6 %reduce-scatter.5.cloned.1.call-done = f32[2048,1024]{1,0:T(8,128)} async-done(((f32[4096,1024]{1,0:T(8,128)}), f32[2048,1024]{1,0:T(8,128)}) %reduce-scatter.5.cloned.1.call-update) | async-done | bytes 8388624 | tf_op jit(solution)/shard_map/reduce_scatter | solution.py:129
  492.8 5.7 fusion.89
  505.5 104.1 %all-gather.7.cloned.1.call-done = bf16[4096,1024]{1,0:T(8,128)(2,1)} async-done(((bf16[2048,1024]{1,0:T(8,128)(2,1)}), bf16[4096,1024]{1,0:T(8,128)(2,1)}) %all-gather.7.cloned.1.call-update) | async-done | bytes 8388624 | tf_op jit(solution)/shard_map/all_gather | solution.py:135
  609.6 92.1 %multiply_convert_fusion.1 = (bf16[4096,2048]{1,0:T(8,128)(2,1)S(1)}, f32[4096,2048]{1,0:T(8,128)}, f32[4096,2048]{1,0:T(8,128)}) fusion(f32[2048]{0:T(1024)S(1)} %convert_element_type.181, bf16[4096,1024]{1,0:T(8,128)(2,1)} %all-gather.7.cloned.1.call-done, bf16[1024,2048]{1,0:T(8,128)(2,1)} %param.34), kind=kOutput, calls=%fused_computation.63 | convolution fusion | flops 17733517312 | bytes 96477184 | tf_op jit(solution)/shard_map/dot_general | solution.py:36
  701.6 5.8 copy-done.53
  707.5 19.5 %convolution_convert_fusion = bf16[4096,1024]{1,0:T(8,128)(2,1)} fusion(bf16[4096,2048]{1,0:T(8,128)(2,1)S(1)} %get-tuple-element.278, bf16[2048,1024]{1,0:T(8,128)(2,1)S(1)} %copy-done.48), kind=kOutput, calls=%fused_computation.102 | convolution fusion | flops 17184063488 | bytes 29360128 | tf_op jit(solution)/shard_map/dot_general | solution.py:36
  727.8 98.6 %reduce-scatter.7.cloned.1.call-done = bf16[2048,1024]{1,0:T(8,128)(2,1)} async-done(((bf16[4096,1024]{1,0:T(8,128)(2,1)}), bf16[2048,1024]{1,0:T(8,128)(2,1)}) %reduce-scatter.7.cloned.1.call-update) | async-done | bytes 4194320 | tf_op jit(solution)/shard_map/reduce_scatter | solution.py:138
  826.4 6.1 fusion.87
  839.8 6.2 fusion.86
  852.0 104.1 %all-gather.9.cloned.1.call-done = bf16[4096,1024]{1,0:T(8,128)(2,1)} async-done(((bf16[2048,1024]{1,0:T(8,128)(2,1)}), bf16[4096,1024]{1,0:T(8,128)(2,1)}) %all-gather.9.cloned.1.call-update) | async-done | bytes 8388624 | tf_op jit(solution)/shard_map/all_gather | solution.py:149
  956.1 39.7 %fusion.93 = (bf16[2048]{0:T(1024)(128)(2,1)}, bf16[4096,2048]{1,0:T(8,128)(2,1)}) fusion(f32[4096,2048]{1,0:T(8,128)} %get-tuple-element.279, bf16[4096,1024]{1,0:T(8,128)(2,1)} %all-gather.9.cloned.1.call-done, bf16[2048,1024]{1,0:T(8,128)(2,1)} %param.36, f32[4096,2048]{1,0:T(8,128)} %get-tuple-element.295, f32[2048]{0:T(1024)S(1)} %convert_element_type.181), kind=kOutput, calls=%fused_computation.154 | convolution fusion | flops 17314084864 | bytes 96481280 | tf_op jit(solution)/shard_map/dot_general | solution.py:30
  995.7 23.5 %fusion.65 = bf16[4096,1024]{1,0:T(8,128)(2,1)} fusion(bf16[1024,2048]{1,0:T(8,128)(2,1)} %param.34, bf16[4096,2048]{1,0:T(8,128)(2,1)} %get-tuple-element.297), kind=kOutput, calls=%fused_computation.101 | convolution fusion | flops 17184063488 | bytes 29360128 | tf_op jit(solution)/shard_map/dot_general | solution.py:30
  1019.3 99.3 %reduce-scatter.9.cloned.1.call-done = bf16[2048,1024]{1,0:T(8,128)(2,1)} async-done(((bf16[4096,1024]{1,0:T(8,128)(2,1)}), bf16[2048,1024]{1,0:T(8,128)(2,1)}) %reduce-scatter.9.cloned.1.call-update) | async-done | bytes 4194320 | tf_op jit(solution)/shard_map/reduce_scatter | solution.py:155
  1118.7 9.8 multiply_reduce_fusion.2
  1128.5 8.1 fusion.85
  1142.9 24.1 %fusion.69 = bf16[1024,2048]{1,0:T(8,128)(2,1)} fusion(bf16[4096,1024]{1,0:T(8,128)(2,1)} %all-gather.7.cloned.1.call-done, bf16[4096,2048]{1,0:T(8,128)(2,1)} %get-tuple-element.297), kind=kOutput, calls=%fused_computation.110 | convolution fusion | flops 17181966336 | bytes 29360128 | tf_op jit(solution)/shard_map/dot_general | solution.py:24
  1167.0 23.7 %convolution_convert_fusion.3 = bf16[2048,1024]{1,0:T(8,128)(2,1)} fusion(bf16[4096,2048]{1,0:T(8,128)(2,1)} %copy-done.53, bf16[4096,1024]{1,0:T(8,128)(2,1)} %all-gather.9.cloned.1.call-done), kind=kOutput, calls=%fused_computation.111 | convolution fusion | flops 17181966336 | bytes 29360128 | tf_op jit(solution)/shard_map/dot_general | solution.py:24
  1190.7 56.3 %all-gather.11.cloned.1.call-done = bf16[4096,1024]{1,0:T(8,128)(2,1)} async-done(((bf16[2048,1024]{1,0:T(8,128)(2,1)}), bf16[4096,1024]{1,0:T(8,128)(2,1)}) %all-gather.11.cloned.1.call-update) | async-done | bytes 8388624 | tf_op jit(solution)/shard_map/all_gather | solution.py:165
  1247.0 9.5 convolution_convert_fusion.1
  1256.5 11.1 reshape.203
  1267.7 9.7 copy.85
  1277.4 162.2 %while.29 = (s32[]{:T(128)}, f32[8,512,8,64]{1,3,2,0:T(8,128)}, bf16[8,512,8,64]{1,3,2,0:T(8,128)(2,1)}, f32[8,512,8,64]{1,3,2,0:T(8,128)}, bf16[8,512,8,64]{1,3...) while((s32[]{:T(128)}, f32[8,512,8,64]{1,3,2,0:T(8,128)}, ...), condition=%wide.region_18.19_spmd.clone, body=%wide.region_16.18_spmd.sunk.clone | while | flops 1374154752 | bytes 69852776 | solution.py:168
  1439.6 12.2 fusion.90
  1466.6 9.6 convolution_convert_fusion.4
  1476.2 5.5 fusion.72
  1481.7 5.5 fusion.74
  1487.2 5.5 fusion.73
  1493.9 10.8 fusion.95
  1504.7 8.4 fusion.96
  1513.1 18.7 %add_convert_fusion = bf16[4096,1024]{1,0:T(8,128)(2,1)} fusion(f32[4096,1024]{1,0:T(8,128)} %fusion.95, f32[4096,1024]{1,0:T(8,128)} %fusion.96, bf16[4096,512]{0,1:T(8,128)(2,1)} %bitcast.183, bf16[1024,512]{1,0:T(8,128)(2,1)S(1)} %copy-done.16), kind=kOutput, calls=%fused_computation.77 | convolution fusion | flops 4307550208 | bytes 47185920 | tf_op jit(solution)/shard_map/dot_general | solution.py:30
  1532.6 42.2 %all-reduce = (f32[1024]{0:T(1024)}, f32[1024]{0:T(1024)}, f32[1024]{0:T(1024)}, f32[1024]{0:T(1024)}, f32[1024]{0:T(1024)}, /*index=5*/f32[1024]{0:T(1024)}) all-reduce(f32[1024]{0:T(1024)S(1)} %copy-done.34, f32[1024]{0:T(1024)S(1)} %copy-done.35, f32[1024]{0:T(1024)S(1)} %copy-done.36, ...), channel_id=1, replica_groups=mesh['dp'=16,'tensor'=2] {'dp','tensor'}, use_global_device_ids=true, to_apply=%region_29.30 | all-reduce | flops 6144 | bytes 49152 | tf_op jit(solution)/shard_map/psum | solution.py:219
  1574.9 33.7 %all-reduce.1 = (bf16[512]{0:T(512)(128)(2,1)S(1)}, bf16[512]{0:T(512)(128)(2,1)S(1)}, bf16[2048]{0:T(1024)(128)(2,1)S(1)}) all-reduce(bf16[512]{0:T(512)(128)(2,1)S(1)} %convert_element_type.206, bf16[512]{0:T(512)(128)(2,1)S(1)} %convert_element_type.215, ...), channel_id=1, replica_groups=mesh['dp'=16,'tensor'=2] {'dp'}, use_global_device_ids=true, to_apply=%region_22.23 | all-reduce | flops 3072 | bytes 12288 | tf_op jit(solution)/shard_map/psum | solution.py:210
  1610.4 120.9 %all-reduce.5.cloned.1.call-done = (bf16[1024,512]{0,1:T(8,128)(2,1)}, bf16[1024,512]{0,1:T(8,128)(2,1)}, bf16[1024,512]{0,1:T(8,128)(2,1)}, bf16[512,1024]{1,0:...) async-done(((bf16[1024,512]{0,1:T(8,128)(2,1)}, bf16[1024,512]{0,1:T(8,128)(2,1)}, bf16[1024,512]{0,1:T(8,128)(2,1)}, bf16[512,1024]{1,0:T(8,128)(2,1)}, ...) | async-done | bytes 12582928 | tf_op jit(solution)/shard_map/psum | solution.py:209
  1731.3 6.8 convert_element_type.220
  1750.0 83.6 %reduce-scatter.11.cloned.1.call-done = bf16[2048,1024]{1,0:T(8,128)(2,1)} async-done(((bf16[4096,1024]{1,0:T(8,128)(2,1)}), bf16[2048,1024]{1,0:T(8,128)(2,1)}) %reduce-scatter.11.cloned.1.call-update) | async-done | bytes 4194320 | tf_op jit(solution)/shard_map/reduce_scatter | solution.py:195
  1833.6 7.9 convert_add_fusion
  (280 shorter events, 314.1 us)
Async XLA Ops:
  7.2 288.2 %copy-start = (bf16[512,1024]{1,0:T(8,128)(2,1)S(1)}, bf16[512,1024]{1,0:T(8,128)(2,1)}, u32[]{:S(2)}) copy-start(bf16[512,1024]{1,0:T(8,128)(2,1)} %param.30) | copy-start | bytes 3145732
  7.2 6.7 copy-start.46
  7.2 109.1 %copy-start.15 = (bf16[1024,512]{1,0:T(8,128)(2,1)S(1)}, bf16[1024,512]{1,0:T(8,128)(2,1)}, u32[]{:S(2)}) copy-start(bf16[1024,512]{1,0:T(8,128)(2,1)} %param.28) | copy-start | bytes 3145732
  7.2 109.1 %all-gather.5.cloned.1.call-start = ((), (), s32[]{:S(2)}) async-start(), calls=%async_computation.4 | async-start | bytes 12582912 | tf_op jit(solution)/shard_map/all_gather | solution.py:118
  8.0 484.9 %reduce-scatter.5.cloned.1.call-start = ((), (), s32[]{:S(2)}) async-start(), calls=%async_computation.5 | async-start | bytes 25165824 | tf_op jit(solution)/shard_map/reduce_scatter | solution.py:129
  136.9 9.8 copy-start.49
  167.3 9.8 copy-start.51
  286.4 7.0 copy-start.24
  303.5 306.0 %all-gather.7.cloned.1.call-start = ((), (), s32[]{:S(2)}) async-start(), calls=%async_computation.6 | async-start | bytes 12582912 | tf_op jit(solution)/shard_map/all_gather | solution.py:135
  498.6 3.4 copy-start.1
  498.6 4.0 copy-start.30
  498.6 4.0 copy-start.38
  498.6 3.4 copy-start.20
  505.4 321.0 %reduce-scatter.7.cloned.1.call-start = ((), (), s32[]{:S(2)}) async-start(), calls=%async_computation.7 | async-start | bytes 12582912 | tf_op jit(solution)/shard_map/reduce_scatter | solution.py:138
  609.6 97.9 %copy-start.48 = (bf16[2048,1024]{1,0:T(8,128)(2,1)S(1)}, bf16[2048,1024]{1,0:T(8,128)(2,1)}, u32[]{:S(2)}) copy-start(bf16[2048,1024]{1,0:T(8,128)(2,1)} %param.36) | copy-start | bytes 12582916
  701.6 5.8 copy-start.53
  727.0 99.5 %copy-start.21 = (f32[2048]{0:T(1024)S(1)}, f32[2048]{0:T(1024)}, u32[]{:S(2)}) copy-start(f32[2048]{0:T(1024)} %copy-done.20) | copy-start | bytes 24580
  727.0 99.5 %copy-start.23 = (f32[2048]{0:T(1024)S(1)}, f32[2048]{0:T(1024)}, u32[]{:S(2)}) copy-start(f32[2048]{0:T(1024)} %copy-done.22) | copy-start | bytes 24580
  727.0 99.4 %copy-start.31 = (f32[1024]{0:T(1024)S(1)}, f32[1024]{0:T(1024)}, u32[]{:S(2)}) copy-start(f32[1024]{0:T(1024)} %param.32) | copy-start | bytes 12292
  727.0 99.4 %copy-start.39 = (f32[1024]{0:T(1024)S(1)}, f32[1024]{0:T(1024)}, u32[]{:S(2)}) copy-start(f32[1024]{0:T(1024)} %param.33) | copy-start | bytes 12292
  727.0 229.1 %all-gather.9.cloned.1.call-start = ((), (), s32[]{:S(2)}) async-start(), calls=%async_computation.8 | async-start | bytes 12582912 | tf_op jit(solution)/shard_map/all_gather | solution.py:149
  833.7 6.1 copy-start.43
  846.0 3.4 copy-start.2
  851.9 266.8 %reduce-scatter.9.cloned.1.call-start = ((), (), s32[]{:S(2)}) async-start(), calls=%async_computation.9 | async-start | bytes 12582912 | tf_op jit(solution)/shard_map/reduce_scatter | solution.py:155
  1019.3 109.2 %copy-start.29 = (f32[2048]{0:T(1024)S(1)}, f32[2048]{0:T(1024)}, u32[]{:S(2)}) copy-start(f32[2048]{0:T(1024)} %copy-done.28) | copy-start | bytes 24580
  1019.3 227.7 %all-gather.11.cloned.1.call-start = ((), (), s32[]{:S(2)}) async-start(), calls=%async_computation.10 | async-start | bytes 12582912 | tf_op jit(solution)/shard_map/all_gather | solution.py:165
  1118.7 9.8 copy-start.8
  1136.6 3.2 copy-start.3
  1136.6 6.2 copy-start.26
  1142.8 588.5 %all-reduce.5.cloned.1.call-start = ((), (), s32[]{:S(2)}) async-start(), calls=%async_computation.12 | async-start | bytes 25165824 | tf_op jit(solution)/shard_map/psum | solution.py:209
  1267.7 9.7 copy-start.25
  1456.6 19.5 %copy-start.12 = (bf16[64,8,8,512]{3,1,2,0:T(8,128)(2,1)}, bf16[64,8,8,512]{3,1,2,0:T(8,128)(2,1)S(1)}, u32[]{:S(2)}) copy-start(bf16[64,8,8,512]{3,1,2,0:T(8,128)(2,1)S(1)} %copy.106) | copy-start | bytes 12582916
  1456.6 4.8 copy-start.5
  1461.4 20.2 %copy-start.6 = (bf16[64,8,8,512]{3,1,2,0:T(8,128)(2,1)}, bf16[64,8,8,512]{3,1,2,0:T(8,128)(2,1)S(1)}, u32[]{:S(2)}) copy-start(bf16[64,8,8,512]{3,1,2,0:T(8,128)(2,1)S(1)} %copy.108) | copy-start | bytes 12582916
  1461.5 5.1 copy-start.11
  1464.2 11.9 slice-start
  1466.5 20.6 %copy-start.13 = (bf16[64,8,8,512]{3,1,2,0:T(8,128)(2,1)}, bf16[64,8,8,512]{3,1,2,0:T(8,128)(2,1)S(1)}, u32[]{:S(2)}) copy-start(bf16[64,8,8,512]{3,1,2,0:T(8,128)(2,1)S(1)} %copy.107) | copy-start | bytes 12582916
  1466.5 9.6 slice-start.1
  1492.7 12.0 copy-start.52
  1492.7 340.9 %reduce-scatter.11.cloned.1.call-start = ((), (), s32[]{:S(2)}) async-start(), calls=%async_computation.11 | async-start | bytes 12582912 | tf_op jit(solution)/shard_map/reduce_scatter | solution.py:195
  1493.9 10.8 copy-start.14
  1504.7 8.4 copy-start.16
  1531.9 43.0 %copy-start.42 = (bf16[2048]{0:T(1024)(128)(2,1)S(1)}, bf16[2048]{0:T(1024)(128)(2,1)}, u32[]{:S(2)}) copy-start(bf16[2048]{0:T(1024)(128)(2,1)} %get-tuple-element.296) | copy-start | bytes 12292
  1731.3 6.8 copy-start.9
  1738.1 4.5 copy-start.19
  1738.1 8.7 copy-start.18
  1738.1 10.3 copy-start.17
  1742.7 91.0 %copy-start.27 = (f32[2048]{0:T(1024)S(1)}, f32[2048]{0:T(1024)}, u32[]{:S(2)}) copy-start(f32[2048]{0:T(1024)} %copy-done.26) | copy-start | bytes 24580
  (17 other events, 19.9 us)
Sparse Core Ops, SparseCore 0:
  9.6 106.6 all-gather.4
  303.7 189.1 reduce-scatter.4
  505.5 103.9 all-gather.6
  727.1 99.2 reduce-scatter.6
  852.0 103.9 all-gather.8
  1019.4 99.2 reduce-scatter.8
  1142.9 103.9 all-gather.10
  1492.8 238.4 all-reduce.4
  1734.3 99.2 reduce-scatter.10
where the time goes:
time: 1860 us; the launch traced here: 1850 us
  waiting for transfers between devices  959 us (52%)
  matrix products  523 us (28%)
  local copies, waits for them, and re-layouts  143 us (8%)
  other arithmetic  132 us (7%)
  blocking collectives  75.9 us (4%)
    reduce_scatter x1, waiting for transfers between devices, shards(): lax.psum_scatter(matmul(mixed, out_weight), 'tensor', scatter_dimension=0...  189 us
    dot_general x6, matrix products, matmul(): return jnp.dot(left, right, preferred_element_type=jnp.float32)  148 us
    psum x1, waiting for transfers between devices, shards(): lax.psum(wgrad_query.astype(jnp.bfloat16), 'dp').astype(jnp.float32)  121 us
    dot_general x6, matrix products, contract_cols(): lax.dot_general(left, right, (((1,), (1,)), ((), ())), preferred_element_...  111 us
    all_gather x1, waiting for transfers between devices, shards(): grad_branch = lax.all_gather(grad_second_low, 'tensor', axis=0, tiled=True)  104 us
    all_gather x1, waiting for transfers between devices, shards(): hidden_all = lax.all_gather(hidden_low, 'tensor', axis=0, tiled=True)  104 us
    all_gather x1, waiting for transfers between devices, shards(): gathered = lax.all_gather(tokens, 'tensor', axis=0, tiled=True)  102 us
    reduce_scatter x1, waiting for transfers between devices, shards(): lax.psum_scatter(contract_cols(grad_inner_low, up_weight).astype(jnp.bflo...  99.3 us
  transfers between devices with their start and end apart: 9, of which 9 were waited for; matrix products, arithmetic and copies ran while one was open for 6% of the time, Pallas kernels for 0%

commit v1 on v0

v1 whole, which is shorter than its diff:
```python
import jax
import jax.numpy as jnp
from jax import lax
from jax.experimental import pallas as pl
from jax.experimental.pallas import tpu as pltpu
from jax.sharding import PartitionSpec as P

HEAD_DIM = 64
SEQ_LEN = 512
LANES = 128
SCALE = HEAD_DIM ** (-0.5)


epsilon = 1e-12
low = jnp.bfloat16
wide = jnp.float32


def contract_rows(left, right):
    return lax.dot_general(left, right, (((0,), (0,)), ((), ())), preferred_element_type=wide)


def contract_cols(left, right):
    return lax.dot_general(left, right, (((1,), (1,)), ((), ())), preferred_element_type=wide)


def matmul(left, right):
    return jnp.dot(left, right, preferred_element_type=wide)


def center(summed):
    middle = jnp.mean(summed, axis=-1, keepdims=True)
    centred = summed - middle
    spread = jnp.mean(centred * centred, axis=-1, keepdims=True)
    scale = lax.rsqrt(spread + epsilon)
    return centred * scale, scale


def center_back(normed, scale, gain, grad):
    scaled = gain * grad
    mean_scaled = jnp.mean(scaled, axis=-1, keepdims=True)
    mean_both = jnp.mean(scaled * normed, axis=-1, keepdims=True)
    return (scaled - mean_scaled - normed * mean_both) * scale


def head_masks():
    column = lax.broadcasted_iota(jnp.int32, (1, LANES), 1)
    return [
        (column // HEAD_DIM == head).astype(wide).astype(low) for head in range(LANES // HEAD_DIM)
    ]


def attend_kernel(lengths_ref, query_ref, key_ref, value_ref, mixed_ref):
    length = lengths_ref[pl.program_id(1)]
    key_id = lax.broadcasted_iota(jnp.int32, (1, SEQ_LEN), 1)
    shut = jnp.where(key_id < length, 0.0, -1e30)
    queries = query_ref[...] * jnp.asarray(SCALE, low)
    keys = key_ref[...]
    values = value_ref[...]
    mixed = None
    for mask in head_masks():
        scores = contract_cols(queries * mask, keys) + shut
        raised = jnp.exp(scores - jnp.max(scores, axis=-1, keepdims=True))
        total = jnp.sum(raised, axis=-1, keepdims=True)
        part = matmul(raised.astype(low), values * mask) * (1.0 / total)
        mixed = part if mixed is None else mixed + part
    mixed_ref[...] = mixed.astype(low)


def attend_back_kernel(
    lengths_ref,
    query_ref,
    key_ref,
    value_ref,
    grad_ref,
    grad_query_ref,
    grad_key_ref,
    grad_value_ref,
    query_sum_ref,
    value_sum_ref,
):
    length = lengths_ref[pl.program_id(1)]
    key_id = lax.broadcasted_iota(jnp.int32, (SEQ_LEN, 1), 0)
    shut = jnp.where(key_id < length, 0.0, -1e30)
    queries = query_ref[...] * jnp.asarray(SCALE, low)
    keys = key_ref[...]
    keys_scaled = keys * jnp.asarray(SCALE, low)
    values = value_ref[...]
    grads = grad_ref[...]
    grad_query = grad_key = grad_value = 0.0
    for mask in head_masks():
        head_queries = queries * mask
        head_grads = grads * mask
        scores = contract_cols(keys, head_queries) + shut
        raised = jnp.exp(scores - jnp.max(scores, axis=0, keepdims=True))
        probs = raised * (1.0 / jnp.sum(raised, axis=0, keepdims=True))
        grad_probs = contract_cols(values, head_grads)
        both = jnp.sum(grad_probs * probs, axis=0, keepdims=True)
        grad_scores = (probs * (grad_probs - both)).astype(low)
        grad_value += matmul(probs.astype(low), head_grads)
        grad_key += matmul(grad_scores, head_queries)
        grad_query += contract_rows(grad_scores, keys_scaled * mask)
    grad_query_ref[...] = grad_query.astype(low)
    grad_key_ref[...] = grad_key.astype(low)
    grad_value_ref[...] = grad_value.astype(low)

    @pl.when(pl.program_id(1) == 0)
    def _():
        query_sum_ref[...] = jnp.zeros_like(query_sum_ref)
        value_sum_ref[...] = jnp.zeros_like(value_sum_ref)

    query_sum_ref[...] += jnp.sum(grad_query, axis=0, keepdims=True)
    value_sum_ref[...] += jnp.sum(grad_value, axis=0, keepdims=True)


def block_specs():
    rows = pl.BlockSpec((SEQ_LEN, LANES), lambda j, i: (i, j))
    sums = pl.BlockSpec((1, LANES), lambda j, i: (0, j))
    return pl.BlockSpec(memory_space=pltpu.SMEM), rows, sums


def attend(lengths, queries, keys, values):
    rows, width = queries.shape
    scalars, block, _ = block_specs()
    pairs = rows * width * SEQ_LEN
    return pl.pallas_call(
        attend_kernel,
        grid=(width // LANES, rows // SEQ_LEN),
        in_specs=[scalars] + [block] * 3,
        out_specs=block,
        out_shape=jax.ShapeDtypeStruct((rows, width), low),
        compiler_params=pltpu.CompilerParams(vmem_limit_bytes=32 * 2**20),
        cost_estimate=pl.CostEstimate(
            flops=16 * pairs, bytes_accessed=8 * rows * width, transcendentals=pairs // HEAD_DIM
        ),
    )(lengths, queries, keys, values)


def attend_back(lengths, queries, keys, values, grads):
    rows, width = queries.shape
    scalars, block, sums = block_specs()
    pairs = rows * width * SEQ_LEN
    return pl.pallas_call(
        attend_back_kernel,
        grid=(width // LANES, rows // SEQ_LEN),
        in_specs=[scalars] + [block] * 4,
        out_specs=[block] * 3 + [sums] * 2,
        out_shape=[jax.ShapeDtypeStruct((rows, width), low)] * 3
        + [jax.ShapeDtypeStruct((1, width), wide)] * 2,
        compiler_params=pltpu.CompilerParams(vmem_limit_bytes=32 * 2**20),
        cost_estimate=pl.CostEstimate(
            flops=40 * pairs, bytes_accessed=14 * rows * width, transcendentals=pairs // HEAD_DIM
        ),
    )(lengths, queries, keys, values, grads)


def sharing(dp, tensor):
    if tensor == 2 and dp % 2 == 0:
        over = [(0, 1), (1, 0)]
        mates = [(i, i ^ 1) for i in range(dp)]
        lane = lambda: lax.axis_index("dp") % 2

        def spread(weight, axis):
            half = weight.shape[axis] // 2
            mine = lax.dynamic_slice_in_dim(weight, lane() * half, half, axis)
            fetched = lax.ppermute(mine, "tensor", over)
            passed = lax.ppermute(fetched, "dp", mates)
            return [weight, jnp.concatenate([fetched, passed], axis=axis)]

        def spread_vector(vector):
            half = vector.shape[0] // 2
            other = lax.ppermute(vector, "tensor", over)
            return [vector, jnp.where(lane() == 0, other, jnp.roll(other, half))]

        def collect(grads, axis):
            own, other = grads
            half = other.shape[axis] // 2
            first, last = jnp.split(other, 2, axis=axis)
            arrived = lax.ppermute(last.astype(low), "dp", mates)
            summed = (first + arrived.astype(wide)).astype(low)
            term = lax.ppermute(summed, "tensor", over).astype(wide)
            left, right = jnp.split(own, 2, axis=axis)
            return jnp.concatenate(
                [
                    (left + jnp.where(lane() == 0, term, 0.0)).astype(low),
                    (right + jnp.where(lane() == 1, term, 0.0)).astype(low),
                ],
                axis=axis,
            )

        def order(sums):
            own, other = sums
            half = other.shape[0] // 2
            other = jnp.where(lane() == 0, other, jnp.roll(other, half))
            whole = jnp.stack([own, other])
            return jnp.where(lax.axis_index("tensor") == 0, whole, whole[::-1]).reshape(-1)

    else:

        def spread(weight, axis):
            return [lax.all_gather(weight, "tensor", axis=axis, tiled=True)]

        def spread_vector(vector):
            return [lax.all_gather(vector, "tensor", axis=0, tiled=True)]

        def collect(grads, axis):
            return lax.psum_scatter(
                grads[0].astype(low), "tensor", scatter_dimension=axis, tiled=True
            )

        def order(sums):
            return sums[0]

    return spread, spread_vector, collect, order


def make_shards(dp, tensor):
    spread, spread_vector, collect, order = sharing(dp, tensor)

    def shards(
        tokens,
        lengths,
        cotangent,
        query_weight,
        query_bias,
        key_weight,
        value_weight,
        value_bias,
        out_weight,
        out_bias,
        first_gain,
        first_shift,
        up_weight,
        up_bias,
        down_weight,
        down_bias,
        second_gain,
        second_shift,
    ):
        rows = tokens.shape[0]
        slots = rows // SEQ_LEN
        place = lax.axis_index("tensor")
        my_lengths = lax.dynamic_slice_in_dim(lengths[0], place * slots, slots, 0)
        row_live = (
            jnp.arange(SEQ_LEN, dtype=jnp.int32)[None, :] < my_lengths[:, None]
        ).astype(wide).reshape(rows, 1)

        query_parts = spread(query_weight, 1)
        key_parts = spread(key_weight, 1)
        value_parts = spread(value_weight, 1)
        out_parts = spread(out_weight, 0)
        up_parts = spread(up_weight, 1)
        down_parts = spread(down_weight, 0)
        query_biases = spread_vector(query_bias)
        value_biases = spread_vector(value_bias)
        up_biases = spread_vector(up_bias)
        pieces = range(len(query_parts))

        attended = []
        attn_sum = 0.0
        for i in pieces:
            queries = (matmul(tokens, query_parts[i]) + query_biases[i].astype(wide)).astype(low)
            keys = matmul(tokens, key_parts[i]).astype(low)
            values = (matmul(tokens, value_parts[i]) + value_biases[i].astype(wide)).astype(low)
            mixed = attend(my_lengths, queries, keys, values)
            attended.append((queries, keys, values, mixed))
            attn_sum += matmul(mixed, out_parts[i])
        first_sum = tokens.astype(wide) + attn_sum + out_bias.astype(wide)
        first_normed, first_scale = center(first_sum)
        hidden = first_normed * first_gain + first_shift
        hidden_low = hidden.astype(low)

        branch = 0.0
        inner_parts = []
        for i in pieces:
            inner = matmul(hidden_low, up_parts[i]) + up_biases[i].astype(wide)
            phi = 0.5 + 0.5 * lax.erf(inner * 0.5**0.5)
            slope = phi + inner * (jnp.exp(inner * inner * -0.5) * 0.3989422804014327)
            active = (inner * phi).astype(low)
            inner_parts.append((active, slope.astype(low)))
            branch += matmul(active, down_parts[i])
        second_sum = hidden + branch + down_bias.astype(wide)
        second_normed, second_scale = center(second_sum)
        layer_out = second_normed * second_gain + second_shift

        grad_out = cotangent.astype(wide) * row_live
        grad_second = center_back(second_normed, second_scale, second_gain, grad_out)
        ggrad_second = jnp.sum(grad_out * second_normed, axis=0)
        sgrad_second = jnp.sum(grad_out, axis=0)
        bgrad_down = jnp.sum(grad_second, axis=0)
        grad_second_low = grad_second.astype(low)

        grads_down, grads_up, sums_up = [None] * 2, [None] * 2, [None] * 2
        back_hidden = 0.0
        for i in reversed(pieces):
            active, slope = inner_parts[i]
            grads_down[i] = contract_rows(active, grad_second_low)
            grad_inner = contract_cols(grad_second_low, down_parts[i]) * slope.astype(wide)
            sums_up[i] = jnp.sum(grad_inner, axis=0)
            grad_inner = grad_inner.astype(low)
            grads_up[i] = contract_rows(hidden_low, grad_inner)
            back_hidden += contract_cols(grad_inner, up_parts[i])
        wgrad_down = collect(grads_down, 0)
        wgrad_up = collect(grads_up, 1)
        wgrad_down = lax.psum(wgrad_down, "dp")

        grad_hidden = grad_second + back_hidden
        grad_first = center_back(first_normed, first_scale, first_gain, grad_hidden)
        ggrad_first = jnp.sum(grad_hidden * first_normed, axis=0)
        sgrad_first = jnp.sum(grad_hidden, axis=0)
        bgrad_out = jnp.sum(grad_first, axis=0)
        grad_first_low = grad_first.astype(low)

        grads_out, grads_query, grads_key, grads_value = ([None] * 2 for _ in range(4))
        sums_query, sums_value = [None] * 2, [None] * 2
        grad_tokens = grad_first
        for i in reversed(pieces):
            queries, keys, values, mixed = attended[i]
            grads_out[i] = contract_rows(mixed, grad_first_low)
            grad_mixed = contract_cols(grad_first_low, out_parts[i]).astype(low)
            grad_query, grad_key, grad_value, query_sum, value_sum = attend_back(
                my_lengths, queries, keys, values, grad_mixed
            )
            sums_query[i] = query_sum[0]
            sums_value[i] = value_sum[0]
            grads_query[i] = contract_rows(tokens, grad_query)
            grads_key[i] = contract_rows(tokens, grad_key)
            grads_value[i] = contract_rows(tokens, grad_value)
            grad_tokens += (
                contract_cols(grad_query, query_parts[i])
                + contract_cols(grad_key, key_parts[i])
                + contract_cols(grad_value, value_parts[i])
            )
        wgrad_out = collect(grads_out, 0)
        wgrad_up, wgrad_out, wgrad_down = lax.optimization_barrier(
            (wgrad_up, wgrad_out, wgrad_down)
        )
        wgrad_up, wgrad_out = lax.psum((wgrad_up, wgrad_out), "dp")
        last = [collect(grads, 1) for grads in (grads_query, grads_key, grads_value)]
        *last, wgrad_up, wgrad_out = lax.optimization_barrier((*last, wgrad_up, wgrad_out))
        wgrad_query, wgrad_key, wgrad_value = lax.psum(tuple(last), "dp")

        vectors = [order(sums) for sums in (sums_query, sums_value, sums_up)]
        vectors += [
            bgrad_out,
            ggrad_first,
            sgrad_first,
            bgrad_down,
            ggrad_second,
            sgrad_second,
        ]
        edges, size = [], 0
        for vector in vectors[:-1]:
            size += vector.shape[0]
            edges.append(size)
        vectors = jnp.split(lax.psum(jnp.concatenate(vectors), ("dp", "tensor")), edges)
        for i in range(3):
            share = vectors[i].shape[0] // tensor
            vectors[i] = lax.dynamic_slice_in_dim(vectors[i], place * share, share, 0)
        (
            bgrad_query,
            bgrad_value,
            bgrad_up,
            bgrad_out,
            ggrad_first,
            sgrad_first,
            bgrad_down,
            ggrad_second,
            sgrad_second,
        ) = vectors
        return (
            layer_out,
            grad_tokens,
            wgrad_query.astype(wide),
            bgrad_query,
            wgrad_key.astype(wide),
            wgrad_value.astype(wide),
            bgrad_value,
            wgrad_out.astype(wide),
            bgrad_out,
            ggrad_first,
            sgrad_first,
            wgrad_up.astype(wide),
            bgrad_up,
            wgrad_down.astype(wide),
            bgrad_down,
            ggrad_second,
            sgrad_second,
        )

    return shards


def solution(mesh):
    return jax.shard_map(
        make_shards(mesh.shape["dp"], mesh.shape["tensor"]),
        mesh=mesh,
        in_specs=(
            P(("dp", "tensor"), None),
            P("dp", None),
            P(("dp", "tensor"), None),
            P(None, "tensor"),
            P("tensor"),
            P(None, "tensor"),
            P(None, "tensor"),
            P("tensor"),
            P("tensor", None),
            P(),
            P(),
            P(),
            P(None, "tensor"),
            P("tensor"),
            P("tensor", None),
            P(),
            P(),
            P(),
        ),
        out_specs=(
            P(("dp", "tensor"), None),
            P(("dp", "tensor"), None),
            P(None, "tensor"),
            P("tensor"),
            P(None, "tensor"),
            P(None, "tensor"),
            P("tensor"),
            P("tensor", None),
            P(),
            P(),
            P(),
            P(None, "tensor"),
            P("tensor"),
            P("tensor", None),
            P(),
            P(),
            P(),
        ),
        check_vma=False,
    )
```

time: 1860 us -> 1050 us (0.56)
  waiting for transfers between devices: 959 us -> 347 us
  matrix products: 523 us -> 329 us
  Pallas kernels: 0 us -> 128 us
  local copies, waits for them, and re-layouts: 143 us -> 85.9 us
  other arithmetic: 132 us -> 75.6 us
  blocking collectives: 75.9 us -> 41.2 us
  starting transfers between devices: 0.37 us -> 20.6 us
    reduce_scatter x4 -> x0, waiting for transfers between devices: 470 us -> none  [the longest x1 189 us: shards(): lax.psum_scatter(matmul(mixed, out_weight), 'tensor', scatter_dimension=0...]
    all_gather x4 -> x0, waiting for transfers between devices: 367 us -> none  [the longest x1 104 us: shards(): grad_branch = lax.all_gather(grad_second_low, 'tensor', axis=0, tiled=True)]
    dot_general x62 -> x12, matrix products: 339 us -> 93.4 us  [matmul(): return jnp.dot(left, right, preferred_element_type=wide)]
    ppermute x0 -> x27, waiting for transfers between devices: none -> 163 us  [the longest x6 111 us: collect(): term = lax.ppermute(summed, 'tensor', over).astype(wide)]
    pallas_call x0 -> x4, Pallas kernels: none -> 128 us  [the longest x2 89.4 us: attend_back(): pl.pallas_call(attend_back_kernel, grid=(width // LANES, rows // SEQ_LEN)...]
    psum x1 -> x3, waiting for transfers between devices: 121 us -> 184 us  [the longest x1 85.6 us: shards(): wgrad_down = lax.psum(wgrad_down, 'dp')]
    reduce_sum x18 -> x4, other arithmetic: 71.3 us -> 17.6 us  [the longest x1 7.77 us: shards(): ggrad_second = jnp.sum(grad_out * second_normed, axis=0)]
    reshape x4 -> x0, local copies, waits for them, and re-layouts: 44.6 us -> none  [split_heads(): return rows.reshape(SEQS, SEQ_LEN, local_heads, HEAD_DIM)]
  transfers between devices with their start and end apart: 9 -> 30, of which waited for: 9 -> 12; matrix products, arithmetic and copies ran while one was open for 6% -> 25% of each run, Pallas kernels for 0% -> 4%
where the time goes in v1:
time: 1050 us; the launch traced here: 1040 us
  waiting for transfers between devices  347 us (33%)
  matrix products  329 us (31%)
  Pallas kernels  128 us (12%)
  local copies, waits for them, and re-layouts  85.9 us (8%)
  other arithmetic  75.6 us (7%)
  blocking collectives  41.2 us (4%)
  starting transfers between devices  20.6 us (2%)
  between operations  15.4 us (1%)
    dot_general x12, matrix products, contract_cols(): lax.dot_general(left, right, (((1,), (1,)), ((), ())), preferred_element_...  147 us
    ppermute x6, waiting for transfers between devices, collect(): term = lax.ppermute(summed, 'tensor', over).astype(wide)  111 us
    dot_general x12, matrix products, matmul(): return jnp.dot(left, right, preferred_element_type=wide)  93.4 us
    pallas_call x2, Pallas kernels, attend_back(): pl.pallas_call(attend_back_kernel, grid=(width // LANES, rows // SEQ_LEN)...  89.4 us
    dot_general x12, matrix products, contract_rows(): lax.dot_general(left, right, (((0,), (0,)), ((), ())), preferred_element_...  89.3 us
    psum x1, waiting for transfers between devices, shards(): wgrad_down = lax.psum(wgrad_down, 'dp')  85.6 us
    psum x1, waiting for transfers between devices, shards(): wgrad_query, wgrad_key, wgrad_value = lax.psum(tuple(last), 'dp')  54.4 us
    unnamed x183, local copies, waits for them, and re-layouts  53.5 us
  transfers between devices with their start and end apart: 30, of which 12 were waited for; matrix products, arithmetic and copies ran while one was open for 25% of the time, Pallas kernels for 4%

profile of v1, /device:TPU:0, one launch (start us, length us, event | category | flops | bytes accessed | tf_op | source)
XLA Modules:
  0.0 1043.7 jit_solution(11844913594033701327)
XLA Ops:
  22.9 5.0 convolution_convert_fusion.3.key_ref
  41.7 19.7 %shard_map.305 = bf16[2048,512]{1,0:T(8,128)(2,1)S(1)} custom-call(s32[4]{0:T(128)S(1)} %fusion.44.lengths_ref, bf16[2048,512]{1,0:T(8,128)(2,1)S(1)} %copy-done.18, bf16[2048,512]{1,0:T(8,128)(2,1)S(1)} %convolution_convert_fusion.3.key_ref, bf16[2048,512]{1,0:T(8,128)(2,1)S(1)} %copy-done.16), custom_call_target="tpu_custom_call" | custom-call | flops 8589934592 | bytes 8388608 | tf_op jit(solution)/shard_map/pallas_call | solution.py:126
  62.7 5.8 fusion.64
  68.5 6.4 copy.35
  75.0 6.7 copy.41
  89.0 7.8 collective-permute-done.3
  96.8 11.2 %collective-permute-done = bf16[1024,256]{1,0:T(8,128)(2,1)S(1)} collective-permute-done((bf16[1024,256]{1,0:T(8,128)(2,1)}, bf16[1024,256]{1,0:T(8,128)(2,1)S(1)}, u32[]{:S(2)}, u32[]{:S(2)}) %collective-permute-start) | collective-permute-done | bytes 524320 | tf_op jit(solution)/shard_map/ppermute | solution.py:166
  117.0 19.4 %shard_map.306 = bf16[2048,512]{1,0:T(8,128)(2,1)S(1)} custom-call(s32[4]{0:T(128)S(1)} %fusion.44.lengths_ref, bf16[2048,512]{1,0:T(8,128)(2,1)S(1)} %fusion.18.query_ref, bf16[2048,512]{1,0:T(8,128)(2,1)S(1)} %fusion.20.key_ref, bf16[2048,512]{1,0:T(8,128)(2,1)S(1)} %fusion.19.value_ref), custom_call_target="tpu_custom_call" | custom-call | flops 8589934592 | bytes 8388608 | tf_op jit(solution)/shard_map/pallas_call | solution.py:126
  137.4 5.7 fusion.62
  148.7 13.9 %multiply_convert_fusion.1 = (bf16[2048,2048]{1,0:T(8,128)(2,1)}, f32[2048,2048]{1,0:T(8,128)}) fusion(f32[2048]{0:T(1024)S(1)} %convert_element_type.233, bf16[2048,1024]{0,1:T(8,128)(2,1)S(1)} %fusion.7, bf16[1024,2048]{1,0:T(8,128)(2,1)S(1)} %copy-done.50), kind=kOutput, calls=%fused_computation.6 | convolution fusion | flops 8615100416 | bytes 33562624 | tf_op jit(solution)/shard_map/dot_general | solution.py:28
  162.5 32.9 %collective-permute-done.10 = bf16[1024,1024]{1,0:T(8,128)(2,1)} collective-permute-done((bf16[1024,1024]{1,0:T(8,128)(2,1)}, bf16[1024,1024]{1,0:T(8,128)(2,1)}, u32[]{:S(2)}, u32[]{:S(2)}) %collective-permute-start.10) | collective-permute-done | bytes 2097184 | tf_op jit(solution)/shard_map/ppermute | solution.py:166
  195.4 14.6 %fusion.65 = f32[2048,1024]{0,1:T(8,128)} fusion(bf16[2048,2048]{1,0:T(8,128)(2,1)} %get-tuple-element.126, bf16[2048,1024]{1,0:T(8,128)(2,1)} %param.32), kind=kOutput, calls=%fused_computation.181 | convolution fusion | flops 8589934592 | bytes 20971520 | tf_op jit(solution)/shard_map/dot_general | solution.py:28
  212.7 14.1 %multiply_convert_fusion = (bf16[2048,2048]{1,0:T(8,128)(2,1)}, f32[2048,2048]{1,0:T(8,128)}) fusion(f32[2048]{0:T(1024)S(1)} %fusion.41, bf16[2048,1024]{0,1:T(8,128)(2,1)S(1)} %fusion.7, bf16[1024,2048]{1,0:T(8,128)(2,1)S(1)} %constant_dynamic-update-slice_fusion.8), kind=kOutput, calls=%fused_computation.4 | convolution fusion | flops 8615100416 | bytes 33562624 | tf_op jit(solution)/shard_map/dot_general | solution.py:28
  229.0 19.9 %fusion.63 = (f32[2048]{0:T(1024)S(1)}, f32[2048,1024]{0,1:T(8,128)}) fusion(f32[1024]{0:T(1024)S(1)} %convert_element_type.237, f32[2048,1024]{0,1:T(8,128)} %fusion.65, bf16[2048,2048]{1,0:T(8,128)(2,1)} %get-tuple-element.128, bf16[2048,1024]{1,0:T(8,128)(2,1)} %copy-done.51, f32[1024]{0:T(1024)S(1)} %copy-done.70, f32[1024]{0:T(1024)S(1)} %copy-done.65, ...), kind=kOutput, calls=%fused_computation.179 | convolution fusion | flops 8606709760 | bytes 37785600 | tf_op jit(solution)/shard_map/dot_general | solution.py:28
  259.3 7.8 multiply_reduce_fusion
  267.0 15.4 %fusion.74 = f32[2048,1024]{1,0:T(8,128)} fusion(bf16[2048,2048]{1,0:T(8,128)(2,1)} %get-tuple-element.128, bf16[2048,1024]{0,1:T(8,128)(2,1)S(1)} %get-tuple-element.90), kind=kOutput, calls=%fused_computation.190 | convolution fusion | flops 8589934592 | bytes 20971520 | tf_op jit(solution)/shard_map/dot_general | solution.py:20
  282.5 22.7 %fusion = (f32[2048]{0:T(1024)}, bf16[2048,2048]{1,0:T(8,128)(2,1)}, f32[2048,2048]{1,0:T(8,128)}) fusion(f32[2048,2048]{1,0:T(8,128)} %get-tuple-element.129, f32[2048]{0:T(1024)S(1)} %fusion.41, bf16[2048,1024]{0,1:T(8,128)(2,1)S(1)} %get-tuple-element.90, bf16[2048,1024]{1,0:T(8,128)(2,1)S(1)} %copy-done.52), kind=kOutput, calls=%fused_computation.8 | convolution fusion | flops 8644458496 | bytes 50348032 | tf_op jit(solution)/shard_map/dot_general | solution.py:24
  305.2 22.7 %fusion.2 = (f32[2048]{0:T(1024)}, bf16[2048,2048]{1,0:T(8,128)(2,1)}, f32[2048,2048]{1,0:T(8,128)}) fusion(f32[2048,2048]{1,0:T(8,128)} %get-tuple-element.127, f32[2048]{0:T(1024)S(1)} %convert_element_type.233, bf16[2048,1024]{0,1:T(8,128)(2,1)S(1)} %get-tuple-element.90, bf16[2048,1024]{1,0:T(8,128)(2,1)S(1)} %copy-done.49), kind=kOutput, calls=%fused_computation.10 | convolution fusion | flops 8644458496 | bytes 50348032 | tf_op jit(solution)/shard_map/dot_general | solution.py:24
  327.8 16.9 %fusion.49 = f32[1024,2048]{1,0:T(8,128)} fusion(bf16[2048,1024]{0,1:T(8,128)(2,1)} %copy-done.34, f32[2048,2048]{1,0:T(8,128)} %get-tuple-element.133, bf16[2048,2048]{1,0:T(8,128)(2,1)} %get-tuple-element.89), kind=kOutput, calls=%fused_computation.167 | convolution fusion | flops 8602517504 | bytes 37748736 | tf_op jit(solution)/shard_map/dot_general | solution.py:20
  344.7 17.1 %fusion.47 = f32[2048,1024]{0,1:T(8,128)} fusion(bf16[1024,2048]{1,0:T(8,128)(2,1)} %param.30, f32[2048,2048]{1,0:T(8,128)} %get-tuple-element.132, bf16[2048,2048]{1,0:T(8,128)(2,1)} %get-tuple-element.87), kind=kOutput, calls=%fused_computation.166 | convolution fusion | flops 8602517504 | bytes 37748736 | tf_op jit(solution)/shard_map/dot_general | solution.py:24
  361.9 25.7 %multiply_reduce_fusion.1 = (f32[1024]{0:T(1024)}, f32[2048]{0:T(1024)S(1)}, f32[2048]{0:T(1024)S(1)}, f32[1024]{0:T(1024)}, f32[2048,1024]{0,1:T(8,128)}) fusion(f32[2048,1024]{0,1:T(8,128)S(1)} %bitcast.105, f32[2048]{0:T(1024)S(1)} %add_rsqrt_fusion.1, f32[2048]{0:T(1024)S(1)} %broadcast_multiply_fusion.5, f32[1024]{0:T(1024)S(1)} %copy-done.65, ...), kind=kOutput, calls=%fused_computation.13 | convolution fusion | flops 8644454400 | bytes 67198976 | tf_op jit(solution)/shard_map/dot_general | solution.py:24
  387.6 7.4 fusion.54
  413.4 44.8 %shard_map.307 = (bf16[2048,512]{1,0:T(8,128)(2,1)S(1)}, bf16[2048,512]{1,0:T(8,128)(2,1)S(1)}, bf16[2048,512]{1,0:T(8,128)(2,1)S(1)}, f32[1,512]{1,0:T(1,128)S(1)}, f32[1,512]{1,0:T(1,128)S(1)}) custom-call(s32[4]{0:T(128)S(1)} %copy-done.2, bf16[2048,512]{1,0:T(8,128)(2,1)S(1)} %copy-done.23, bf16[2048,512]{1,0:T(8,128)(2,1)S(1)} %copy-done.15, ...), custom_call_target="tpu_custom_call" | custom-call | flops 21474836480 | bytes 14680064 | tf_op jit(solution)/shard_map/pallas_call | solution.py:143
  461.9 5.7 fusion.67
  471.3 5.7 fusion.66
  477.0 44.6 %shard_map.308 = (bf16[2048,512]{1,0:T(8,128)(2,1)S(1)}, bf16[2048,512]{1,0:T(8,128)(2,1)S(1)}, bf16[2048,512]{1,0:T(8,128)(2,1)S(1)}, f32[1,512]{1,0:T(1,128)S(1)}, f32[1,512]{1,0:T(1,128)S(1)}) custom-call(s32[4]{0:T(128)S(1)} %copy-done.2, bf16[2048,512]{1,0:T(8,128)(2,1)S(1)} %copy-done.19, bf16[2048,512]{1,0:T(8,128)(2,1)S(1)} %copy-done.13, ...), custom_call_target="tpu_custom_call" | custom-call | flops 21474836480 | bytes 14680064 | tf_op jit(solution)/shard_map/pallas_call | solution.py:143
  525.5 5.8 fusion.70
  558.7 15.0 %fusion.45 = f32[1024,2048]{1,0:T(8,128)S(1)} fusion(bf16[2048,1024]{0,1:T(8,128)(2,1)} %copy-done.34, f32[2048,2048]{1,0:T(8,128)} %get-tuple-element.132, bf16[2048,2048]{1,0:T(8,128)(2,1)} %get-tuple-element.87), kind=kOutput, calls=%fused_computation.165 | convolution fusion | flops 8602517504 | bytes 37748736 | tf_op jit(solution)/shard_map/dot_general | solution.py:20
  573.8 5.0 fusion.16
  579.2 5.1 fusion.17
  585.8 11.3 %fusion.73 = f32[2048,1024]{1,0:T(8,128)S(1)} fusion(bf16[2048,2048]{1,0:T(8,128)(2,1)} %get-tuple-element.126, bf16[2048,1024]{0,1:T(8,128)(2,1)S(1)} %copy-done.37), kind=kOutput, calls=%fused_computation.189 | convolution fusion | flops 8589934592 | bytes 20971520 | tf_op jit(solution)/shard_map/dot_general | solution.py:20
  597.1 30.5 %collective-permute-done.26 = bf16[1024,1024]{1,0:T(8,128)(2,1)} collective-permute-done((bf16[1024,1024]{1,0:T(8,128)(2,1)}, bf16[1024,1024]{1,0:T(8,128)(2,1)}, u32[]{:S(2)}, u32[]{:S(2)}) %collective-permute-start.26) | collective-permute-done | bytes 2097184 | tf_op jit(solution)/shard_map/ppermute | solution.py:181
  627.6 44.0 %collective-permute-done.22 = bf16[1024,1024]{1,0:T(8,128)(2,1)} collective-permute-done((bf16[1024,1024]{1,0:T(8,128)(2,1)}, bf16[1024,1024]{1,0:T(8,128)(2,1)}, u32[]{:S(2)}, u32[]{:S(2)}) %collective-permute-start.22) | collective-permute-done | bytes 2097184 | tf_op jit(solution)/shard_map/ppermute | solution.py:181
  671.6 5.8 fusion.9
  680.2 7.8 fusion.69
  689.7 5.8 fusion.68
  695.5 6.8 collective-permute-done.24
  706.2 85.6 %all-reduce.6.cloned.1.call-done = bf16[2048,1024]{1,0:T(8,128)(2,1)} async-done(((bf16[2048,1024]{1,0:T(8,128)(2,1)}), bf16[2048,1024]{1,0:T(8,128)(2,1)}) %all-reduce.6.cloned.1.call-update) | async-done | bytes 4194320 | tf_op jit(solution)/shard_map/psum | solution.py:305
  791.9 41.2 %psum.53 = f32[12288]{0:T(1024)S(1)} all-reduce(f32[12288]{0:T(1024)S(1)} %constant_dynamic-update-slice_fusion.14), channel_id=1, replica_groups=mesh['dp'=16,'tensor'=2] {'dp','tensor'}, use_global_device_ids=true, to_apply=%region_20.21 | all-reduce | flops 12288 | bytes 98304 | tf_op jit(solution)/shard_map/psum | solution.py:356
  844.2 8.9 collective-permute-done.20
  854.5 9.8 collective-permute-done.16
  864.7 10.7 %collective-permute-done.18 = bf16[1024,256]{0,1:T(8,128)(2,1)S(1)} collective-permute-done((bf16[1024,256]{0,1:T(8,128)(2,1)S(1)}, bf16[1024,256]{0,1:T(8,128)(2,1)S(1)}, u32[]{:S(2)}, u32[]{:S(2)}) %collective-permute-start.18) | collective-permute-done | bytes 524320 | tf_op jit(solution)/shard_map/ppermute | solution.py:181
  877.2 44.5 %all-reduce.10.cloned.1.call-done = (bf16[1024,2048]{1,0:T(8,128)(2,1)}, bf16[512,1024]{1,0:T(8,128)(2,1)}) async-done(((bf16[1024,2048]{1,0:T(8,128)(2,1)}, bf16[512,1024]{1,0:T(8,128)(2,1)}), (bf16[1024,2048]{1,0:T(8,128)(2,1)}, bf16[512,1024]{1,0:T(8,128)(2,1)})) %all-reduce.10.cloned.1.call-update) | async-done | bytes 5242896 | tf_op jit(solution)/shard_map/psum | solution.py:338
  921.8 21.6 %add_add_fusion = f32[2048,1024]{0,1:T(8,128)} fusion(f32[2048,1024]{0,1:T(8,128)} %fusion.70, f32[2048,1024]{0,1:T(8,128)} %fusion.68, f32[2048,1024]{0,1:T(8,128)} %fusion.69, f32[2048,1024]{0,1:T(8,128)} %get-tuple-element.85, f32[2048,1024]{0,1:T(8,128)} %fusion.66, f32[2048,1024]{0,1:T(8,128)} %fusion.67, bf16[2048,512]{1,0:T(8,128)(2,1)S(1)} %get-tuple-element.37, ...), kind=kOutput, calls=%fused_computation.14 | convolution fusion | flops 2160066560 | bytes 61865984 | tf_op jit(solution)/shard_map/dot_general | solution.py:24
  943.3 9.3 copy.51
  952.6 9.4 copy.50
  962.6 6.9 convert_element_type.286
  975.5 54.4 %all-reduce.8.cloned.1.call-done = (bf16[1024,512]{0,1:T(8,128)(2,1)}, bf16[1024,512]{0,1:T(8,128)(2,1)}, bf16[1024,512]{0,1:T(8,128)(2,1)}) async-done(((bf16[1024,512]{0,1:T(8,128)(2,1)}, bf16[1024,512]{0,1:T(8,128)(2,1)}, bf16[1024,512]{0,1:T(8,128)(2,1)}), (bf16[1024,512]{0,1:T(8,128)(2,1)}, bf16[1024,512]{0,1:T(8,128)(2,1)}, bf16[1024,512]{0,1:T(8,128)(2,1)})) %all-reduce.8.cloned.1.call-update) | async-done | bytes 3145744 | tf_op jit(solution)/shard_map/psum | solution.py:341
  (326 shorter events, 163.7 us)
Async XLA Ops:
  7.2 784.6 %all-reduce.6.cloned.1.call-start = ((), (), s32[]{:S(2)}) async-start(), calls=%async_computation | async-start | bytes 8388608 | tf_op jit(solution)/shard_map/psum | solution.py:305
  7.3 74.4 %collective-permute-start.2 = (bf16[512]{0:T(512)(128)(2,1)}, bf16[512]{0:T(512)(128)(2,1)S(1)}, u32[]{:S(2)}, u32[]{:S(2)}) collective-permute-start(bf16[512]{0:T(512)(128)(2,1)} %param.22), channel_id=1, source_target_pairs={{0,1},{1,0},{2,3},{3,2},{4,5},{5,4},{6,7},{7,6},{8,9},{9,8},{10,11... | collective-permute-start | bytes 3080 | tf_op jit(solution)/shard_map/ppermute | solution.py:172
  10.3 71.5 %collective-permute-start.7 = (bf16[512]{0:T(512)(128)(2,1)}, bf16[512]{0:T(512)(128)(2,1)S(1)}, u32[]{:S(2)}, u32[]{:S(2)}) collective-permute-start(bf16[512]{0:T(512)(128)(2,1)} %param.25), channel_id=1, source_target_pairs={{0,1},{1,0},{2,3},{3,2},{4,5},{5,4},{6,7},{7,6},{8,9},{9,8},{10,11... | collective-permute-start | bytes 3080 | tf_op jit(solution)/shard_map/ppermute | solution.py:172
  10.3 73.5 %collective-permute-start.12 = (bf16[2048]{0:T(1024)(128)(2,1)}, bf16[2048]{0:T(1024)(128)(2,1)S(1)}, u32[]{:S(2)}, u32[]{:S(2)}) collective-permute-start(bf16[2048]{0:T(1024)(128)(2,1)} %param.31), channel_id=1, source_target_pairs={{0,1},{1,0},{2,3},{3,2},{4,5},{5,4},{6,7},{7,6},{8,9},{9,8},{10,11... | collective-permute-start | bytes 12296 | tf_op jit(solution)/shard_map/ppermute | solution.py:172
  13.1 72.0 %collective-permute-start.8 = (bf16[256,1024]{1,0:T(8,128)(2,1)}, bf16[256,1024]{1,0:T(8,128)(2,1)}, u32[]{:S(2)}, u32[]{:S(2)}) collective-permute-start(bf16[256,1024]{1,0:T(8,128)(2,1)} %constant_dynamic-slice_fusion.2), channel_id=1, source_target_pairs={{0,1},{1,0},{2,3},{3,2},{4,5},{5,4},{6,7},{7,6},{8,9},{9,8},{10,11... | collective-permute-start | bytes 1572872 | tf_op jit(solution)/shard_map/ppermute | solution.py:166
  15.1 68.9 %collective-permute-start.5 = (bf16[1024,256]{1,0:T(8,128)(2,1)}, bf16[1024,256]{1,0:T(8,128)(2,1)}, u32[]{:S(2)}, u32[]{:S(2)}) collective-permute-start(bf16[1024,256]{1,0:T(8,128)(2,1)} %constant_dynamic-slice_fusion.3), channel_id=1, source_target_pairs={{0,1},{1,0},{2,3},{3,2},{4,5},{5,4},{6,7},{7,6},{8,9},{9,8},{10,11... | collective-permute-start | bytes 1572872 | tf_op jit(solution)/shard_map/ppermute | solution.py:166
  19.1 97.9 %copy-start.1 = (s32[4]{0:T(128)}, s32[4]{0:T(128)S(1)}, u32[]{:S(2)}) copy-start(s32[4]{0:T(128)S(1)} %fusion.44.lengths_ref) | copy-start | bytes 52
  81.7 27.0 %copy-start.31 = (bf16[2048,1024]{1,0:T(8,128)(2,1)S(1)}, bf16[2048,1024]{1,0:T(8,128)(2,1)}, u32[]{:S(2)}) copy-start(bf16[2048,1024]{1,0:T(8,128)(2,1)} %param.18) | copy-start | bytes 12582916
  81.7 15.1 %collective-permute-start.3 = (bf16[1024,256]{1,0:T(8,128)(2,1)}, bf16[1024,256]{1,0:T(8,128)(2,1)S(1)}, u32[]{:S(2)}, u32[]{:S(2)}) collective-permute-start(bf16[1024,256]{1,0:T(8,128)(2,1)} %constant_dynamic-slice_fusion.4), channel_id=1, source_target_pairs={{0,1},{1,0},{2,3},{3,2},{4,5},{5,4},{6,7},{7,6},{8,9},{9,8},{10,11... | collective-permute-start | bytes 1572872 | tf_op jit(solution)/shard_map/ppermute | solution.py:166
  81.8 26.2 %collective-permute-start = (bf16[1024,256]{1,0:T(8,128)(2,1)}, bf16[1024,256]{1,0:T(8,128)(2,1)S(1)}, u32[]{:S(2)}, u32[]{:S(2)}) collective-permute-start(bf16[1024,256]{1,0:T(8,128)(2,1)} %constant_dynamic-slice_fusion.5), channel_id=1, source_target_pairs={{0,1},{1,0},{2,3},{3,2},{4,5},{5,4},{6,7},{7,6},{8,9},{9,8},{10,11... | collective-permute-start | bytes 1572872 | tf_op jit(solution)/shard_map/ppermute | solution.py:166
  83.9 126.1 %collective-permute-start.13 = (bf16[1024,1024]{1,0:T(8,128)(2,1)S(1)}, bf16[1024,1024]{1,0:T(8,128)(2,1)S(1)}, u32[]{:S(2)}, u32[]{:S(2)}) collective-permute-start(bf16[1024,1024]{1,0:T(8,128)(2,1)S(1)} %copy-done.43), channel_id=1, source_target_pairs={{0,1},{1,0},{2,3},{3,2},{4,5},{5,4},{6,7},{7,6},{8,9},{9,8},{10,11... | collective-permute-start | bytes 6291464 | tf_op jit(solution)/shard_map/ppermute | solution.py:166
  84.0 24.1 %collective-permute-start.6 = (bf16[1024,256]{1,0:T(8,128)(2,1)}, bf16[1024,256]{1,0:T(8,128)(2,1)S(1)}, u32[]{:S(2)}, u32[]{:S(2)}) collective-permute-start(bf16[1024,256]{1,0:T(8,128)(2,1)} %collective-permute-done.5), channel_id=1, source_target_pairs={{0,2},{2,0},{4,6},{6,4},{8,10},{10,8},{12,14},{14,12},{16,18},{18,... | collective-permute-start | bytes 1572872 | tf_op jit(solution)/shard_map/ppermute | solution.py:167
  85.1 110.2 %collective-permute-start.10 = (bf16[1024,1024]{1,0:T(8,128)(2,1)}, bf16[1024,1024]{1,0:T(8,128)(2,1)}, u32[]{:S(2)}, u32[]{:S(2)}) collective-permute-start(bf16[1024,1024]{1,0:T(8,128)(2,1)} %constant_dynamic-slice_fusion.1), channel_id=1, source_target_pairs={{0,1},{1,0},{2,3},{3,2},{4,5},{5,4},{6,7},{7,6},{8,9},{9,8},{10,11... | collective-permute-start | bytes 6291464 | tf_op jit(solution)/shard_map/ppermute | solution.py:166
  96.8 39.6 %collective-permute-start.9 = (bf16[256,1024]{1,0:T(8,128)(2,1)}, bf16[256,1024]{1,0:T(8,128)(2,1)S(1)}, u32[]{:S(2)}, u32[]{:S(2)}) collective-permute-start(bf16[256,1024]{1,0:T(8,128)(2,1)} %collective-permute-done.8), channel_id=1, source_target_pairs={{0,2},{2,0},{4,6},{6,4},{8,10},{10,8},{12,14},{14,12},{16,18},{18,... | collective-permute-start | bytes 1572872 | tf_op jit(solution)/shard_map/ppermute | solution.py:167
  108.0 3.1 collective-permute-start.4
  108.1 5.4 collective-permute-start.1
  117.0 19.4 %copy-start.22 = (bf16[2048,512]{1,0:T(8,128)(2,1)}, bf16[2048,512]{1,0:T(8,128)(2,1)S(1)}, u32[]{:S(2)}) copy-start(bf16[2048,512]{1,0:T(8,128)(2,1)S(1)} %fusion.18.query_ref) | copy-start | bytes 6291460
  117.0 20.4 %copy-start.35 = (bf16[2048,1024]{0,1:T(8,128)(2,1)S(1)}, bf16[2048,1024]{0,1:T(8,128)(2,1)}, u32[]{:S(2)}) copy-start(bf16[2048,1024]{0,1:T(8,128)(2,1)} %copy.35) | copy-start | bytes 12582916
  148.6 64.1 %copy-start.34 = (bf16[2048,1024]{0,1:T(8,128)(2,1)}, bf16[2048,1024]{0,1:T(8,128)(2,1)S(1)}, u32[]{:S(2)}) copy-start(bf16[2048,1024]{0,1:T(8,128)(2,1)S(1)} %fusion.7) | copy-start | bytes 12582916
  195.4 17.1 %collective-permute-start.11 = (bf16[1024,1024]{1,0:T(8,128)(2,1)}, bf16[1024,1024]{1,0:T(8,128)(2,1)S(1)}, u32[]{:S(2)}, u32[]{:S(2)}) collective-permute-start(bf16[1024,1024]{1,0:T(8,128)(2,1)} %collective-permute-done.10), channel_id=1, source_target_pairs={{0,2},{2,0},{4,6},{6,4},{8,10},{10,8},{12,14},{14,12},{16,18},{18,... | collective-permute-start | bytes 6291464 | tf_op jit(solution)/shard_map/ppermute | solution.py:167
  210.0 16.8 %collective-permute-start.14 = (bf16[1024,1024]{1,0:T(8,128)(2,1)S(1)}, bf16[1024,1024]{1,0:T(8,128)(2,1)S(1)}, u32[]{:S(2)}, u32[]{:S(2)}) collective-permute-start(bf16[1024,1024]{1,0:T(8,128)(2,1)S(1)} %collective-permute-done.13), channel_id=1, source_target_pairs={{0,2},{2,0},{4,6},{6,4},{8,10},{10,8},{12,14},{14,12},{16,18},{18,... | collective-permute-start | bytes 6291464 | tf_op jit(solution)/shard_map/ppermute | solution.py:167
  267.0 38.1 %copy-start.36 = (bf16[2048,1024]{0,1:T(8,128)(2,1)}, bf16[2048,1024]{0,1:T(8,128)(2,1)S(1)}, u32[]{:S(2)}) copy-start(bf16[2048,1024]{0,1:T(8,128)(2,1)S(1)} %get-tuple-element.90) | copy-start | bytes 12582916
  282.5 22.7 %copy-start.49 = (bf16[2048,1024]{1,0:T(8,128)(2,1)S(1)}, bf16[2048,1024]{1,0:T(8,128)(2,1)}, u32[]{:S(2)}) copy-start(bf16[2048,1024]{1,0:T(8,128)(2,1)} %param.32) | copy-start | bytes 12582916
  305.2 56.7 %slice-start = ((s8[8388608]{0:T(1024)(128)(4,1)}), s8[4194304]{0:T(1024)(128)(4,1)S(1)}, s32[]{:S(2)}) async-start(s8[8388608]{0:T(1024)(128)(4,1)} %bitcast.104), calls=%async_computation.3 | async-start | bytes 8388608
  327.8 34.1 %slice-start.1 = ((s8[8388608]{0:T(1024)(128)(4,1)}), s8[4194304]{0:T(1024)(128)(4,1)S(1)}, s32[]{:S(2)}) async-start(s8[8388608]{0:T(1024)(128)(4,1)} %bitcast.104), calls=%async_computation.4 | async-start | bytes 8388608
  413.4 44.8 %copy-start.32 = (bf16[2048,1024]{1,0:T(8,128)(2,1)S(1)}, bf16[2048,1024]{1,0:T(8,128)(2,1)}, u32[]{:S(2)}) copy-start(bf16[2048,1024]{1,0:T(8,128)(2,1)} %param.18) | copy-start | bytes 12582916
  535.2 38.6 %collective-permute-start.25 = (bf16[1024,1024]{1,0:T(8,128)(2,1)}, bf16[1024,1024]{1,0:T(8,128)(2,1)}, u32[]{:S(2)}, u32[]{:S(2)}) collective-permute-start(bf16[1024,1024]{1,0:T(8,128)(2,1)} %split.207), channel_id=1, source_target_pairs={{0,2},{2,0},{4,6},{6,4},{8,10},{10,8},{12,14},{14,12},{16,18},{18,... | collective-permute-start | bytes 6291464 | tf_op jit(solution)/shard_map/ppermute | solution.py:179
  539.6 39.6 %collective-permute-start.21 = (bf16[1024,1024]{1,0:T(8,128)(2,1)}, bf16[1024,1024]{1,0:T(8,128)(2,1)}, u32[]{:S(2)}, u32[]{:S(2)}) collective-permute-start(bf16[1024,1024]{1,0:T(8,128)(2,1)} %split.208), channel_id=1, source_target_pairs={{0,2},{2,0},{4,6},{6,4},{8,10},{10,8},{12,14},{14,12},{16,18},{18,... | collective-permute-start | bytes 6291464 | tf_op jit(solution)/shard_map/ppermute | solution.py:179
  542.2 145.8 %collective-permute-start.23 = (bf16[256,1024]{1,0:T(8,128)(2,1)}, bf16[256,1024]{1,0:T(8,128)(2,1)}, u32[]{:S(2)}, u32[]{:S(2)}) collective-permute-start(bf16[256,1024]{1,0:T(8,128)(2,1)} %split.209), channel_id=1, source_target_pairs={{0,2},{2,0},{4,6},{6,4},{8,10},{10,8},{12,14},{14,12},{16,18},{18,... | collective-permute-start | bytes 1572872 | tf_op jit(solution)/shard_map/ppermute | solution.py:179
  544.7 295.6 %collective-permute-start.15 = (bf16[1024,256]{0,1:T(8,128)(2,1)}, bf16[1024,256]{0,1:T(8,128)(2,1)}, u32[]{:S(2)}, u32[]{:S(2)}) collective-permute-start(bf16[1024,256]{0,1:T(8,128)(2,1)} %split.212), channel_id=1, source_target_pairs={{0,2},{2,0},{4,6},{6,4},{8,10},{10,8},{12,14},{14,12},{16,18},{18,... | collective-permute-start | bytes 1572872 | tf_op jit(solution)/shard_map/ppermute | solution.py:179
  550.8 285.7 %collective-permute-start.19 = (bf16[1024,256]{0,1:T(8,128)(2,1)}, bf16[1024,256]{0,1:T(8,128)(2,1)}, u32[]{:S(2)}, u32[]{:S(2)}) collective-permute-start(bf16[1024,256]{0,1:T(8,128)(2,1)} %split.210), channel_id=1, source_target_pairs={{0,2},{2,0},{4,6},{6,4},{8,10},{10,8},{12,14},{14,12},{16,18},{18,... | collective-permute-start | bytes 1572872 | tf_op jit(solution)/shard_map/ppermute | solution.py:179
  578.8 48.8 %collective-permute-start.26 = (bf16[1024,1024]{1,0:T(8,128)(2,1)}, bf16[1024,1024]{1,0:T(8,128)(2,1)}, u32[]{:S(2)}, u32[]{:S(2)}) collective-permute-start(bf16[1024,1024]{1,0:T(8,128)(2,1)} %fusion.16), channel_id=1, source_target_pairs={{0,1},{1,0},{2,3},{3,2},{4,5},{5,4},{6,7},{7,6},{8,9},{9,8},{10,11... | collective-permute-start | bytes 6291464 | tf_op jit(solution)/shard_map/ppermute | solution.py:181
  584.3 87.3 %collective-permute-start.22 = (bf16[1024,1024]{1,0:T(8,128)(2,1)}, bf16[1024,1024]{1,0:T(8,128)(2,1)}, u32[]{:S(2)}, u32[]{:S(2)}) collective-permute-start(bf16[1024,1024]{1,0:T(8,128)(2,1)} %fusion.17), channel_id=1, source_target_pairs={{0,1},{1,0},{2,3},{3,2},{4,5},{5,4},{6,7},{7,6},{8,9},{9,8},{10,11... | collective-permute-start | bytes 6291464 | tf_op jit(solution)/shard_map/ppermute | solution.py:181
  679.9 241.8 %all-reduce.10.cloned.1.call-start = ((), (), s32[]{:S(2)}) async-start(), calls=%async_computation.2 | async-start | bytes 10485760 | tf_op jit(solution)/shard_map/psum | solution.py:338
  689.2 13.0 %collective-permute-start.24 = (bf16[256,1024]{1,0:T(8,128)(2,1)S(1)}, bf16[256,1024]{1,0:T(8,128)(2,1)S(1)}, u32[]{:S(2)}, u32[]{:S(2)}) collective-permute-start(bf16[256,1024]{1,0:T(8,128)(2,1)S(1)} %fusion.37), channel_id=1, source_target_pairs={{0,1},{1,0},{2,3},{3,2},{4,5},{5,4},{6,7},{7,6},{8,9},{9,8},{10,11... | collective-permute-start | bytes 1572872 | tf_op jit(solution)/shard_map/ppermute | solution.py:181
  706.2 85.7 %copy-start.72 = (f32[1024]{0:T(1024)S(1)}, f32[1024]{0:T(1024)}, u32[]{:S(2)}) copy-start(f32[1024]{0:T(1024)} %get-tuple-element.75) | copy-start | bytes 12292
  706.2 85.7 %copy-start.69 = (f32[1024]{0:T(1024)S(1)}, f32[1024]{0:T(1024)}, u32[]{:S(2)}) copy-start(f32[1024]{0:T(1024)} %get-tuple-element.73) | copy-start | bytes 12292
  706.2 85.7 %copy-start.68 = (f32[1024]{0:T(1024)S(1)}, f32[1024]{0:T(1024)}, u32[]{:S(2)}) copy-start(f32[1024]{0:T(1024)} %get-tuple-element.72) | copy-start | bytes 12292
  706.2 85.7 %copy-start.67 = (f32[1024]{0:T(1024)S(1)}, f32[1024]{0:T(1024)}, u32[]{:S(2)}) copy-start(f32[1024]{0:T(1024)} %get-tuple-element.78) | copy-start | bytes 12292
  791.8 238.1 %all-reduce.8.cloned.1.call-start = ((), (), s32[]{:S(2)}) async-start(), calls=%async_computation.1 | async-start | bytes 6291456 | tf_op jit(solution)/shard_map/psum | solution.py:341
  833.2 20.3 %copy-start.62 = (f32[12288]{0:T(1024)}, f32[12288]{0:T(1024)S(1)}, u32[]{:S(2)}) copy-start(f32[12288]{0:T(1024)S(1)} %psum.53) | copy-start | bytes 147460
  833.2 19.9 %copy-start.39 = (f32[1024,512]{0,1:T(8,128)S(1)}, f32[1024,512]{0,1:T(8,128)}, u32[]{:S(2)}) copy-start(f32[1024,512]{0,1:T(8,128)} %convolution_bitcast_fusion.1) | copy-start | bytes 6291460
  836.4 5.5 collective-permute-start.17
  838.1 15.1 %collective-permute-start.20 = (bf16[1024,256]{0,1:T(8,128)(2,1)S(1)}, bf16[1024,256]{0,1:T(8,128)(2,1)S(1)}, u32[]{:S(2)}, u32[]{:S(2)}) collective-permute-start(bf16[1024,256]{0,1:T(8,128)(2,1)S(1)} %fusion.38), channel_id=1, source_target_pairs={{0,1},{1,0},{2,3},{3,2},{4,5},{5,4},{6,7},{7,6},{8,9},{9,8},{10,11... | collective-permute-start | bytes 1572872 | tf_op jit(solution)/shard_map/ppermute | solution.py:181
  841.9 22.5 %copy-start.42 = (f32[1024,512]{0,1:T(8,128)S(1)}, f32[1024,512]{0,1:T(8,128)}, u32[]{:S(2)}) copy-start(f32[1024,512]{0,1:T(8,128)} %convolution_bitcast_fusion.5) | copy-start | bytes 6291460
  841.9 22.5 %collective-permute-start.16 = (bf16[1024,256]{0,1:T(8,128)(2,1)S(1)}, bf16[1024,256]{0,1:T(8,128)(2,1)S(1)}, u32[]{:S(2)}, u32[]{:S(2)}) collective-permute-start(bf16[1024,256]{0,1:T(8,128)(2,1)S(1)} %fusion.40), channel_id=1, source_target_pairs={{0,1},{1,0},{2,3},{3,2},{4,5},{5,4},{6,7},{7,6},{8,9},{9,8},{10,11... | collective-permute-start | bytes 1572872 | tf_op jit(solution)/shard_map/ppermute | solution.py:181
  842.1 33.3 %copy-start.40 = (f32[1024,512]{0,1:T(8,128)S(1)}, f32[1024,512]{0,1:T(8,128)}, u32[]{:S(2)}) copy-start(f32[1024,512]{0,1:T(8,128)} %convolution_bitcast_fusion.3) | copy-start | bytes 6291460
  842.1 33.3 %collective-permute-start.18 = (bf16[1024,256]{0,1:T(8,128)(2,1)S(1)}, bf16[1024,256]{0,1:T(8,128)(2,1)S(1)}, u32[]{:S(2)}, u32[]{:S(2)}) collective-permute-start(bf16[1024,256]{0,1:T(8,128)(2,1)S(1)} %fusion.39), channel_id=1, source_target_pairs={{0,1},{1,0},{2,3},{3,2},{4,5},{5,4},{6,7},{7,6},{8,9},{9,8},{10,11... | collective-permute-start | bytes 1572872 | tf_op jit(solution)/shard_map/ppermute | solution.py:181
  (62 other events, 351.8 us)
Sparse Core Ops, SparseCore 0:
  680.0 111.7 all-reduce.5
  796.7 124.9 all-reduce.9
  926.2 103.6 all-reduce.7

commit v2 on v1

--- a/solution.py
+++ b/solution.py
@@ -22,6 +22,9 @@
 
 def contract_cols(left, right):
     return lax.dot_general(left, right, (((1,), (1,)), ((), ())), preferred_element_type=wide)
+
+
+hold = lax.optimization_barrier
 
 
 def matmul(left, right):
@@ -172,13 +175,16 @@
             other = lax.ppermute(vector, "tensor", over)
             return [vector, jnp.where(lane() == 0, other, jnp.roll(other, half))]
 
-        def collect(grads, axis):
-            own, other = grads
-            half = other.shape[axis] // 2
-            first, last = jnp.split(other, 2, axis=axis)
-            arrived = lax.ppermute(last.astype(low), "dp", mates)
-            summed = (first + arrived.astype(wide)).astype(low)
-            term = lax.ppermute(summed, "tensor", over).astype(wide)
+        def pass_on(other, axis):
+            return lax.ppermute(jnp.split(other, 2, axis=axis)[1], "dp", mates)
+
+        def send_back(other, arrived, axis):
+            first = jnp.split(other, 2, axis=axis)[0]
+            summed = (first.astype(wide) + arrived.astype(wide)).astype(low)
+            return lax.ppermute(summed, "tensor", over)
+
+        def finish(own, term, axis):
+            term = term.astype(wide)
             left, right = jnp.split(own, 2, axis=axis)
             return jnp.concatenate(
                 [
@@ -203,19 +209,25 @@
         def spread_vector(vector):
             return [lax.all_gather(vector, "tensor", axis=0, tiled=True)]
 
-        def collect(grads, axis):
+        def pass_on(other, axis):
+            return None
+
+        def send_back(other, arrived, axis):
+            return None
+
+        def finish(own, term, axis):
             return lax.psum_scatter(
-                grads[0].astype(low), "tensor", scatter_dimension=axis, tiled=True
+                own.astype(low), "tensor", scatter_dimension=axis, tiled=True
             )
 
         def order(sums):
             return sums[0]
 
-    return spread, spread_vector, collect, order
+    return spread, spread_vector, pass_on, send_back, finish, order
 
 
 def make_shards(dp, tensor):
-    spread, spread_vector, collect, order = sharing(dp, tensor)
+    spread, spread_vector, pass_on, send_back, finish, order = sharing(dp, tensor)
 
     def shards(
         tokens,
@@ -292,6 +304,7 @@
 
         grads_down, grads_up, sums_up = [None] * 2, [None] * 2, [None] * 2
         back_hidden = 0.0
+        ffn_arrived = [None] * 2
         for i in reversed(pieces):
             active, slope = inner_parts[i]
             grads_down[i] = contract_rows(active, grad_second_low)
@@ -300,9 +313,17 @@
             grad_inner = grad_inner.astype(low)
             grads_up[i] = contract_rows(hidden_low, grad_inner)
             back_hidden += contract_cols(grad_inner, up_parts[i])
-        wgrad_down = collect(grads_down, 0)
-        wgrad_up = collect(grads_up, 1)
-        wgrad_down = lax.psum(wgrad_down, "dp")
+            if i == 1:
+                grads_down[1], grads_up[1] = grads_down[1].astype(low), grads_up[1].astype(low)
+                grads_down[1], grads_up[1], grad_second_low = hold(
+                    (grads_down[1], grads_up[1], grad_second_low)
+                )
+                ffn_arrived = [pass_on(grads_down[1], 0), pass_on(grads_up[1], 1)]
+        back_hidden, ffn_arrived = hold((back_hidden, ffn_arrived))
+        ffn_terms = [
+            send_back(grads_down[1], ffn_arrived[0], 0),
+            send_back(grads_up[1], ffn_arrived[1], 1),
+        ]
 
         grad_hidden = grad_second + back_hidden
         grad_first = center_back(first_normed, first_scale, first_gain, grad_hidden)
@@ -314,13 +335,32 @@
         grads_out, grads_query, grads_key, grads_value = ([None] * 2 for _ in range(4))
         sums_query, sums_value = [None] * 2, [None] * 2
         grad_tokens = grad_first
+        kinds = (grads_out, grads_query, grads_key, grads_value)
+        axes = (0, 1, 1, 1)
+        arrived = [None] * 4
+        terms = [None] * 4
         for i in reversed(pieces):
+            if i == 0:
+                wgrad_down = finish(grads_down[0], ffn_terms[0], 0)
+                wgrad_up = finish(grads_up[0], ffn_terms[1], 1)
+                wgrad_down, wgrad_up, grad_first_low = hold(
+                    (wgrad_down, wgrad_up, grad_first_low)
+                )
+                wgrad_down, wgrad_up = lax.psum((wgrad_down, wgrad_up), "dp")
             queries, keys, values, mixed = attended[i]
             grads_out[i] = contract_rows(mixed, grad_first_low)
             grad_mixed = contract_cols(grad_first_low, out_parts[i]).astype(low)
             grad_query, grad_key, grad_value, query_sum, value_sum = attend_back(
                 my_lengths, queries, keys, values, grad_mixed
             )
+            if i == 0:
+                grad_query, grad_key, grad_value, arrived = hold(
+                    (grad_query, grad_key, grad_value, arrived)
+                )
+                terms = [
+                    send_back(grads[1], got, axis)
+                    for grads, got, axis in zip(kinds, arrived, axes)
+                ]
             sums_query[i] = query_sum[0]
             sums_value[i] = value_sum[0]
             grads_query[i] = contract_rows(tokens, grad_query)
@@ -331,14 +371,18 @@
                 + contract_cols(grad_key, key_parts[i])
                 + contract_cols(grad_value, value_parts[i])
             )
-        wgrad_out = collect(grads_out, 0)
-        wgrad_up, wgrad_out, wgrad_down = lax.optimization_barrier(
-            (wgrad_up, wgrad_out, wgrad_down)
-        )
-        wgrad_up, wgrad_out = lax.psum((wgrad_up, wgrad_out), "dp")
-        last = [collect(grads, 1) for grads in (grads_query, grads_key, grads_value)]
-        *last, wgrad_up, wgrad_out = lax.optimization_barrier((*last, wgrad_up, wgrad_out))
-        wgrad_query, wgrad_key, wgrad_value = lax.psum(tuple(last), "dp")
+            if i == 1:
+                for grads in kinds:
+                    grads[1] = grads[1].astype(low)
+                others, ffn_terms, grad_first_low = hold(
+                    ([grads[1] for grads in kinds], ffn_terms, grad_first_low)
+                )
+                for grads, other in zip(kinds, others):
+                    grads[1] = other
+                arrived = [pass_on(other, axis) for other, axis in zip(others, axes)]
+        last = [finish(grads[0], term, axis) for grads, term, axis in zip(kinds, terms, axes)]
+        last, wgrad_down, wgrad_up = hold((last, wgrad_down, wgrad_up))
+        wgrad_out, wgrad_query, wgrad_key, wgrad_value = lax.psum(tuple(last), "dp")
 
         vectors = [order(sums) for sums in (sums_query, sums_value, sums_up)]
         vectors += [
@@ -353,7 +397,8 @@
         for vector in vectors[:-1]:
             size += vector.shape[0]
             edges.append(size)
-        vectors = jnp.split(lax.psum(jnp.concatenate(vectors), ("dp", "tensor")), edges)
+        joined, _ = hold((jnp.concatenate(vectors), [grads[0] for grads in kinds]))
+        vectors = jnp.split(lax.psum(joined, ("dp", "tensor")), edges)
         for i in range(3):
             share = vectors[i].shape[0] // tensor
             vectors[i] = lax.dynamic_slice_in_dim(vectors[i], place * share, share, 0)

time: 1050 us -> 950 us (0.905)
  waiting for transfers between devices: 347 us -> 236 us
  other arithmetic: 75.6 us -> 87.4 us
    psum x3 -> x2, waiting for transfers between devices: 184 us -> 135 us  [the longest x1 73.9 us: shards(): wgrad_out, wgrad_query, wgrad_key, wgrad_value = lax.psum(tuple(last), 'dp')]
    ppermute x12, waiting for transfers between devices: 111 us -> 62.3 us  [the longest x6 62.2 us: send_back(): return lax.ppermute(summed, 'tensor', over)]
    ppermute x6, waiting for transfers between devices: 51.8 us -> 38.1 us  [spread(): fetched = lax.ppermute(mine, 'tensor', over)]
    unnamed x183 -> x245, local copies, waits for them, and re-layouts: 53.5 us -> 61.5 us
    convert_element_type x11 -> x12, other arithmetic: 21.6 us -> 28.5 us  [the longest x6 14 us: send_back(): summed = (first.astype(wide) + arrived.astype(wide)).astype(low)]
  transfers between devices with their start and end apart: 30 -> 29, of which waited for: 12 -> 8; matrix products, arithmetic and copies ran while one was open for 25% -> 27% of each run, Pallas kernels for 4% -> 4%
where the time goes in v2:
time: 950 us; the launch traced here: 944 us
  matrix products  323 us (34%)
  waiting for transfers between devices  236 us (25%)
  Pallas kernels  128 us (13%)
  other arithmetic  87.4 us (9%)
  local copies, waits for them, and re-layouts  84.2 us (9%)
  blocking collectives  48.6 us (5%)
  starting transfers between devices  20.2 us (2%)
  between operations  16.1 us (2%)
    dot_general x12, matrix products, contract_cols(): lax.dot_general(left, right, (((1,), (1,)), ((), ())), preferred_element_...  139 us
    dot_general x12, matrix products, matmul(): return jnp.dot(left, right, preferred_element_type=wide)  93.4 us
    dot_general x12, matrix products, contract_rows(): lax.dot_general(left, right, (((0,), (0,)), ((), ())), preferred_element_...  90.5 us
    pallas_call x2, Pallas kernels, attend_back(): pl.pallas_call(attend_back_kernel, grid=(width // LANES, rows // SEQ_LEN)...  89.3 us
    psum x1, waiting for transfers between devices, shards(): wgrad_out, wgrad_query, wgrad_key, wgrad_value = lax.psum(tuple(last), 'dp')  73.9 us
    ppermute x6, waiting for transfers between devices, send_back(): return lax.ppermute(summed, 'tensor', over)  62.2 us
    unnamed x245, local copies, waits for them, and re-layouts  61.5 us
    psum x1, waiting for transfers between devices, shards(): wgrad_down, wgrad_up = lax.psum((wgrad_down, wgrad_up), 'dp')  61.4 us
  transfers between devices with their start and end apart: 29, of which 8 were waited for; matrix products, arithmetic and copies ran while one was open for 27% of the time, Pallas kernels for 4%

profile of v2, /device:TPU:0, one launch (start us, length us, event | category | flops | bytes accessed | tf_op | source)
XLA Modules:
  0.0 943.7 jit_solution(7895616450883369949)
XLA Ops:
  22.2 5.0 convolution_convert_fusion.5.key_ref
  38.0 19.4 %shard_map.305 = bf16[2048,512]{1,0:T(8,128)(2,1)S(1)} custom-call(s32[4]{0:T(128)S(1)} %fusion.41.lengths_ref, bf16[2048,512]{1,0:T(8,128)(2,1)S(1)} %copy-done.19, bf16[2048,512]{1,0:T(8,128)(2,1)S(1)} %convolution_convert_fusion.5.key_ref, bf16[2048,512]{1,0:T(8,128)(2,1)S(1)} %copy-done.17), custom_call_target="tpu_custom_call" | custom-call | flops 8589934592 | bytes 8388608 | tf_op jit(solution)/shard_map/pallas_call | solution.py:129
  58.7 5.8 fusion.62
  67.9 6.4 copy.35
  74.4 6.5 copy.41
  87.4 8.6 collective-permute-done.3
  96.1 11.2 %collective-permute-done.8 = bf16[256,1024]{1,0:T(8,128)(2,1)S(1)} collective-permute-done((bf16[256,1024]{1,0:T(8,128)(2,1)}, bf16[256,1024]{1,0:T(8,128)(2,1)S(1)}, u32[]{:S(2)}, u32[]{:S(2)}) %collective-permute-start.8) | collective-permute-done | bytes 524320 | tf_op jit(solution)/shard_map/ppermute | solution.py:169
  115.9 19.6 %shard_map.306 = bf16[2048,512]{1,0:T(8,128)(2,1)S(1)} custom-call(s32[4]{0:T(128)S(1)} %fusion.41.lengths_ref, bf16[2048,512]{1,0:T(8,128)(2,1)S(1)} %fusion.16.query_ref, bf16[2048,512]{1,0:T(8,128)(2,1)S(1)} %fusion.18.key_ref, bf16[2048,512]{1,0:T(8,128)(2,1)S(1)} %fusion.17.value_ref), custom_call_target="tpu_custom_call" | custom-call | flops 8589934592 | bytes 8388608 | tf_op jit(solution)/shard_map/pallas_call | solution.py:129
  136.5 5.7 fusion.60
  147.8 13.9 %multiply_convert_fusion.1 = (bf16[2048,2048]{1,0:T(8,128)(2,1)}, f32[2048,2048]{1,0:T(8,128)}) fusion(f32[2048]{0:T(1024)S(1)} %convert_element_type.272, bf16[2048,1024]{0,1:T(8,128)(2,1)S(1)} %fusion.7, bf16[1024,2048]{1,0:T(8,128)(2,1)S(1)} %copy-done.61), kind=kOutput, calls=%fused_computation.6 | convolution fusion | flops 8615100416 | bytes 33562624 | tf_op jit(solution)/shard_map/dot_general | solution.py:31
  161.7 14.6 %fusion.63 = f32[2048,1024]{0,1:T(8,128)} fusion(bf16[2048,2048]{1,0:T(8,128)(2,1)} %get-tuple-element.176, bf16[2048,1024]{1,0:T(8,128)(2,1)} %param.32), kind=kOutput, calls=%fused_computation.175 | convolution fusion | flops 8589934592 | bytes 20971520 | tf_op jit(solution)/shard_map/dot_general | solution.py:31
  176.3 18.3 %collective-permute-done.13 = bf16[1024,1024]{1,0:T(8,128)(2,1)} collective-permute-done((bf16[1024,1024]{1,0:T(8,128)(2,1)S(1)}, bf16[1024,1024]{1,0:T(8,128)(2,1)}, u32[]{:S(2)}, u32[]{:S(2)}) %collective-permute-start.13) | collective-permute-done | bytes 2097184 | tf_op jit(solution)/shard_map/ppermute | solution.py:169
  196.9 14.1 %multiply_convert_fusion = (bf16[2048,2048]{1,0:T(8,128)(2,1)}, f32[2048,2048]{1,0:T(8,128)}) fusion(f32[2048]{0:T(1024)S(1)} %fusion.38, bf16[2048,1024]{0,1:T(8,128)(2,1)S(1)} %fusion.7, bf16[1024,2048]{1,0:T(8,128)(2,1)S(1)} %constant_dynamic-update-slice_fusion.8), kind=kOutput, calls=%fused_computation.4 | convolution fusion | flops 8615100416 | bytes 33562624 | tf_op jit(solution)/shard_map/dot_general | solution.py:31
  213.1 19.9 %fusion.61 = (f32[2048]{0:T(1024)S(1)}, f32[2048,1024]{0,1:T(8,128)}) fusion(f32[1024]{0:T(1024)S(1)} %convert_element_type.276, f32[2048,1024]{0,1:T(8,128)} %fusion.63, bf16[2048,2048]{1,0:T(8,128)(2,1)} %get-tuple-element.178, bf16[2048,1024]{1,0:T(8,128)(2,1)} %copy-done.63, f32[1024]{0:T(1024)S(1)} %copy-done.94, f32[1024]{0:T(1024)S(1)} %copy-done.92, ...), kind=kOutput, calls=%fused_computation.173 | convolution fusion | flops 8606709760 | bytes 37785600 | tf_op jit(solution)/shard_map/dot_general | solution.py:31
  238.8 4.6 fusion.6
  248.1 10.8 %convolution_convert_fusion.1 = bf16[2048,1024]{1,0:T(8,128)(2,1)} fusion(bf16[2048,2048]{1,0:T(8,128)(2,1)S(1)} %bitcast.124, bf16[2048,1024]{0,1:T(8,128)(2,1)S(1)} %fusion.50), kind=kOutput, calls=%fused_computation.54 | convolution fusion | flops 8592031744 | bytes 16777216 | tf_op jit(solution)/shard_map/dot_general | solution.py:20
  258.9 21.8 %fusion = (f32[2048]{0:T(1024)S(1)}, bf16[2048,2048]{1,0:T(8,128)(2,1)}, f32[2048,2048]{1,0:T(8,128)}) fusion(f32[2048,2048]{1,0:T(8,128)} %get-tuple-element.179, f32[2048]{0:T(1024)S(1)} %fusion.38, bf16[2048,1024]{0,1:T(8,128)(2,1)S(1)} %fusion.50, bf16[2048,1024]{1,0:T(8,128)(2,1)S(1)} %copy-done.64), kind=kOutput, calls=%fused_computation.8 | convolution fusion | flops 8644458496 | bytes 50348032 | tf_op jit(solution)/shard_map/dot_general | solution.py:24
  280.7 15.0 %convolution_convert_fusion = bf16[1024,2048]{1,0:T(8,128)(2,1)} fusion(bf16[2048,1024]{0,1:T(8,128)(2,1)S(1)} %copy-done.43, f32[2048,2048]{1,0:T(8,128)} %get-tuple-element.182, bf16[2048,2048]{1,0:T(8,128)(2,1)} %get-tuple-element.134), kind=kOutput, calls=%fused_computation.53 | convolution fusion | flops 8604614656 | bytes 33554432 | tf_op jit(solution)/shard_map/dot_general | solution.py:20
  295.7 22.3 %fusion.2 = (f32[2048]{0:T(1024)S(1)}, bf16[2048,2048]{1,0:T(8,128)(2,1)}, f32[2048,2048]{1,0:T(8,128)}) fusion(f32[2048,2048]{1,0:T(8,128)} %get-tuple-element.177, f32[2048]{0:T(1024)S(1)} %convert_element_type.272, bf16[2048,1024]{0,1:T(8,128)(2,1)S(1)} %fusion.50, bf16[2048,1024]{1,0:T(8,128)(2,1)} %param.32), kind=kOutput, calls=%fused_computation.10 | convolution fusion | flops 8644458496 | bytes 50348032 | tf_op jit(solution)/shard_map/dot_general | solution.py:24
  318.1 15.8 %fusion.42 = f32[1024,2048]{1,0:T(8,128)} fusion(bf16[2048,1024]{0,1:T(8,128)(2,1)S(1)} %copy-done.43, f32[2048,2048]{1,0:T(8,128)} %get-tuple-element.183, bf16[2048,2048]{1,0:T(8,128)(2,1)} %get-tuple-element.132), kind=kOutput, calls=%fused_computation.159 | convolution fusion | flops 8602517504 | bytes 37748736 | tf_op jit(solution)/shard_map/dot_general | solution.py:20
  333.9 15.8 %fusion.44 = f32[2048,1024]{0,1:T(8,128)} fusion(bf16[1024,2048]{1,0:T(8,128)(2,1)S(1)} %copy-done.62, f32[2048,2048]{1,0:T(8,128)} %get-tuple-element.183, bf16[2048,2048]{1,0:T(8,128)(2,1)} %get-tuple-element.132), kind=kOutput, calls=%fused_computation.160 | convolution fusion | flops 8602517504 | bytes 37748736 | tf_op jit(solution)/shard_map/dot_general | solution.py:24
  349.6 19.6 %convolution_add_fusion = f32[2048,1024]{0,1:T(8,128)} fusion(f32[2048,1024]{0,1:T(8,128)} %fusion.44, bf16[1024,2048]{1,0:T(8,128)(2,1)} %copy-done.65, f32[2048,2048]{1,0:T(8,128)} %get-tuple-element.182, bf16[2048,2048]{1,0:T(8,128)(2,1)} %get-tuple-element.134), kind=kOutput, calls=%fused_computation.55 | convolution fusion | flops 8604614656 | bytes 46137344 | tf_op jit(solution)/shard_map/dot_general | solution.py:24
  375.2 14.7 %fusion.66 = f32[2048,1024]{1,0:T(8,128)} fusion(bf16[2048,2048]{1,0:T(8,128)(2,1)} %get-tuple-element.176, bf16[2048,1024]{0,1:T(8,128)(2,1)} %copy-done.44), kind=kOutput, calls=%fused_computation.178 | convolution fusion | flops 8589934592 | bytes 20971520 | tf_op jit(solution)/shard_map/dot_general | solution.py:20
  390.0 14.2 %multiply_reduce_fusion = (f32[1024]{0:T(1024)S(1)}, f32[1024]{0:T(1024)S(1)}, f32[1024]{0:T(1024)S(1)}, f32[1024]{0:T(1024)S(1)}, f32[2048]{0:T(1024)S(1)}, /*i...) fusion(bf16[2048,1024]{0,1:T(8,128)(2,1)S(1)} %copy-done.29, ...), kind=kLoop, calls=%fused_computation.12 | loop fusion | flops 52419584 | bytes 46243840 | tf_op jit(solution)/shard_map/reduce_sum | solution.py:300
  404.2 5.4 fusion.51
  413.1 4.6 convolution_convert_fusion.4.grad_ref
  417.7 44.8 %shard_map.307 = (bf16[2048,512]{1,0:T(8,128)(2,1)S(1)}, bf16[2048,512]{1,0:T(8,128)(2,1)S(1)}, bf16[2048,512]{1,0:T(8,128)(2,1)S(1)}, f32[1,512]{1,0:T(1,128)S(1)}, f32[1,512]{1,0:T(1,128)S(1)}) custom-call(s32[4]{0:T(128)S(1)} %copy-done.2, bf16[2048,512]{1,0:T(8,128)(2,1)S(1)} %copy-done.22, bf16[2048,512]{1,0:T(8,128)(2,1)S(1)} %copy-done.16, ...), custom_call_target="tpu_custom_call" | custom-call | flops 21474836480 | bytes 14680064 | tf_op jit(solution)/shard_map/pallas_call | solution.py:146
  465.9 5.7 fusion.64
  480.0 5.7 fusion.65
  485.8 9.4 copy.50
  495.2 6.3 fusion.20
  508.3 16.2 %collective-permute-done.18 = bf16[1024,1024]{1,0:T(8,128)(2,1)} collective-permute-done((bf16[1024,1024]{1,0:T(8,128)(2,1)}, bf16[1024,1024]{1,0:T(8,128)(2,1)}, u32[]{:S(2)}, u32[]{:S(2)}) %collective-permute-start.18) | collective-permute-done | bytes 2097184 | tf_op jit(solution)/shard_map/ppermute | solution.py:184
  524.4 44.6 %collective-permute-done.17 = bf16[1024,1024]{1,0:T(8,128)(2,1)} collective-permute-done((bf16[1024,1024]{1,0:T(8,128)(2,1)}, bf16[1024,1024]{1,0:T(8,128)(2,1)}, u32[]{:S(2)}, u32[]{:S(2)}) %collective-permute-start.17) | collective-permute-done | bytes 2097184 | tf_op jit(solution)/shard_map/ppermute | solution.py:184
  569.0 5.9 fusion.9
  574.9 4.7 pad_maximum_fusion.1
  582.0 4.7 convolution_convert_fusion.3.grad_ref
  586.8 44.4 %shard_map.308 = (bf16[2048,512]{1,0:T(8,128)(2,1)S(1)}, bf16[2048,512]{1,0:T(8,128)(2,1)S(1)}, bf16[2048,512]{1,0:T(8,128)(2,1)S(1)}, f32[1,512]{1,0:T(1,128)S(1)}, f32[1,512]{1,0:T(1,128)S(1)}) custom-call(s32[4]{0:T(128)S(1)} %copy-done.2, bf16[2048,512]{1,0:T(8,128)(2,1)S(1)} %copy-done.20, bf16[2048,512]{1,0:T(8,128)(2,1)S(1)} %copy-done.14, ...), custom_call_target="tpu_custom_call" | custom-call | flops 21474836480 | bytes 14680064 | tf_op jit(solution)/shard_map/pallas_call | solution.py:146
  640.4 6.6 fusion.70
  650.7 5.8 fusion.69
  662.6 5.8 fusion.67
  668.4 5.8 fusion.68
  684.2 48.6 %psum.52 = f32[12288]{0:T(1024)S(1)} all-reduce(f32[12288]{0:T(1024)S(1)} %constant_dynamic-update-slice_fusion.14), channel_id=1, replica_groups=mesh['dp'=16,'tensor'=2] {'dp','tensor'}, use_global_device_ids=true, to_apply=%region_19.20 | all-reduce | flops 12288 | bytes 98304 | tf_op jit(solution)/shard_map/psum | solution.py:401
  749.4 61.4 %all-reduce.7.cloned.1.call-done = (bf16[2048,1024]{1,0:T(8,128)(2,1)}, bf16[1024,2048]{1,0:T(8,128)(2,1)}) async-done(((bf16[2048,1024]{1,0:T(8,128)(2,1)}, bf16[1024,2048]{1,0:T(8,128)(2,1)}), (bf16[2048,1024]{1,0:T(8,128)(2,1)}, bf16[1024,2048]{1,0:T(8,128)(2,1)})) %all-reduce.7.cloned.1.call-update) | async-done | bytes 8388624 | tf_op jit(solution)/shard_map/psum | solution.py:349
  810.8 21.8 %add_add_fusion = f32[2048,1024]{0,1:T(8,128)} fusion(f32[2048,1024]{0,1:T(8,128)} %fusion.69, f32[2048,1024]{0,1:T(8,128)} %fusion.67, f32[2048,1024]{0,1:T(8,128)} %fusion.68, f32[2048,1024]{0,1:T(8,128)} %copy-done.27, f32[2048,1024]{0,1:T(8,128)} %fusion.64, f32[2048,1024]{0,1:T(8,128)} %fusion.65, bf16[2048,512]{1,0:T(8,128)(2,1)S(1)} %get-tuple-element.63, ...), kind=kOutput, calls=%fused_computation.14 | convolution fusion | flops 2160066560 | bytes 61865984 | tf_op jit(solution)/shard_map/dot_general | solution.py:24
  832.5 9.3 copy.51
  842.5 6.9 convert_element_type.339
  849.3 4.4 convert_element_type.340
  853.8 73.9 %all-reduce.5.cloned.1.call-done = (bf16[1024,512]{0,1:T(8,128)(2,1)}, bf16[1024,512]{0,1:T(8,128)(2,1)}, bf16[1024,512]{0,1:T(8,128)(2,1)}, bf16[512,1024]{1,0:T(8,128)(2,1)}) async-done(((bf16[1024,512]{0,1:T(8,128)(2,1)}, bf16[1024,512]{0,1:T(8,128)(2,1)}, bf16[1024,512]{0,1:T(8,128)(2,1)}, bf16[512,1024]{1,0:T(8,128)(2,1)}), (bf16[1024,512]{0,1:T(8,128)(2,1)}, bf16[1024,512]{0,1:T(8,128)(2,1)}, ...) | async-done | bytes 4194320 | tf_op jit(solution)/shard_map/psum | solution.py:385
  (391 shorter events, 151.5 us)
Async XLA Ops:
  7.2 803.5 %all-reduce.7.cloned.1.call-start = ((), (), s32[]{:S(2)}) async-start(), calls=%async_computation.1 | async-start | bytes 16777216 | tf_op jit(solution)/shard_map/psum | solution.py:349
  9.2 74.0 %collective-permute-start = (bf16[1024,256]{1,0:T(8,128)(2,1)}, bf16[1024,256]{1,0:T(8,128)(2,1)}, u32[]{:S(2)}, u32[]{:S(2)}) collective-permute-start(bf16[1024,256]{1,0:T(8,128)(2,1)} %constant_dynamic-slice_fusion.5), channel_id=1, source_target_pairs={{0,1},{1,0},{2,3},{3,2},{4,5},{5,4},{6,7},{7,6},{8,9},{9,8},{10,11... | collective-permute-start | bytes 1572872 | tf_op jit(solution)/shard_map/ppermute | solution.py:169
  12.2 68.8 %collective-permute-start.2 = (bf16[512]{0:T(512)(128)(2,1)}, bf16[512]{0:T(512)(128)(2,1)S(1)}, u32[]{:S(2)}, u32[]{:S(2)}) collective-permute-start(bf16[512]{0:T(512)(128)(2,1)} %param.22), channel_id=1, source_target_pairs={{0,1},{1,0},{2,3},{3,2},{4,5},{5,4},{6,7},{7,6},{8,9},{9,8},{10,11... | collective-permute-start | bytes 3080 | tf_op jit(solution)/shard_map/ppermute | solution.py:175
  14.1 70.3 %collective-permute-start.5 = (bf16[1024,256]{1,0:T(8,128)(2,1)}, bf16[1024,256]{1,0:T(8,128)(2,1)}, u32[]{:S(2)}, u32[]{:S(2)}) collective-permute-start(bf16[1024,256]{1,0:T(8,128)(2,1)} %constant_dynamic-slice_fusion.3), channel_id=1, source_target_pairs={{0,1},{1,0},{2,3},{3,2},{4,5},{5,4},{6,7},{7,6},{8,9},{9,8},{10,11... | collective-permute-start | bytes 1572872 | tf_op jit(solution)/shard_map/ppermute | solution.py:169
  16.1 65.0 %collective-permute-start.7 = (bf16[512]{0:T(512)(128)(2,1)}, bf16[512]{0:T(512)(128)(2,1)S(1)}, u32[]{:S(2)}, u32[]{:S(2)}) collective-permute-start(bf16[512]{0:T(512)(128)(2,1)} %param.25), channel_id=1, source_target_pairs={{0,1},{1,0},{2,3},{3,2},{4,5},{5,4},{6,7},{7,6},{8,9},{9,8},{10,11... | collective-permute-start | bytes 3080 | tf_op jit(solution)/shard_map/ppermute | solution.py:175
  16.1 67.0 %collective-permute-start.12 = (bf16[2048]{0:T(1024)(128)(2,1)}, bf16[2048]{0:T(1024)(128)(2,1)S(1)}, u32[]{:S(2)}, u32[]{:S(2)}) collective-permute-start(bf16[2048]{0:T(1024)(128)(2,1)} %param.31), channel_id=1, source_target_pairs={{0,1},{1,0},{2,3},{3,2},{4,5},{5,4},{6,7},{7,6},{8,9},{9,8},{10,11... | collective-permute-start | bytes 12296 | tf_op jit(solution)/shard_map/ppermute | solution.py:175
  34.8 81.1 %copy-start.1 = (s32[4]{0:T(128)}, s32[4]{0:T(128)S(1)}, u32[]{:S(2)}) copy-start(s32[4]{0:T(128)S(1)} %fusion.41.lengths_ref) | copy-start | bytes 52
  74.4 169.0 %copy-start.80 = (f32[1,4,4,128]{3,1,2,0:T(4,128)}, f32[1,4,4,128]{3,1,2,0:T(4,128)S(1)}, u32[]{:S(2)}) copy-start(f32[1,4,4,128]{3,1,2,0:T(4,128)S(1)} %copy.68) | copy-start | bytes 24580
  80.9 27.7 %copy-start.37 = (bf16[2048,1024]{1,0:T(8,128)(2,1)S(1)}, bf16[2048,1024]{1,0:T(8,128)(2,1)}, u32[]{:S(2)}) copy-start(bf16[2048,1024]{1,0:T(8,128)(2,1)} %param.18) | copy-start | bytes 12582916
  80.9 15.1 %collective-permute-start.3 = (bf16[1024,256]{1,0:T(8,128)(2,1)}, bf16[1024,256]{1,0:T(8,128)(2,1)S(1)}, u32[]{:S(2)}, u32[]{:S(2)}) collective-permute-start(bf16[1024,256]{1,0:T(8,128)(2,1)} %constant_dynamic-slice_fusion.4), channel_id=1, source_target_pairs={{0,1},{1,0},{2,3},{3,2},{4,5},{5,4},{6,7},{7,6},{8,9},{9,8},{10,11... | collective-permute-start | bytes 1572872 | tf_op jit(solution)/shard_map/ppermute | solution.py:169
  81.0 26.2 %collective-permute-start.8 = (bf16[256,1024]{1,0:T(8,128)(2,1)}, bf16[256,1024]{1,0:T(8,128)(2,1)S(1)}, u32[]{:S(2)}, u32[]{:S(2)}) collective-permute-start(bf16[256,1024]{1,0:T(8,128)(2,1)} %constant_dynamic-slice_fusion.2), channel_id=1, source_target_pairs={{0,1},{1,0},{2,3},{3,2},{4,5},{5,4},{6,7},{7,6},{8,9},{9,8},{10,11... | collective-permute-start | bytes 1572872 | tf_op jit(solution)/shard_map/ppermute | solution.py:169
  83.1 78.6 %collective-permute-start.10 = (bf16[1024,1024]{1,0:T(8,128)(2,1)}, bf16[1024,1024]{1,0:T(8,128)(2,1)S(1)}, u32[]{:S(2)}, u32[]{:S(2)}) collective-permute-start(bf16[1024,1024]{1,0:T(8,128)(2,1)} %constant_dynamic-slice_fusion.1), channel_id=1, source_target_pairs={{0,1},{1,0},{2,3},{3,2},{4,5},{5,4},{6,7},{7,6},{8,9},{9,8},{10,11... | collective-permute-start | bytes 6291464 | tf_op jit(solution)/shard_map/ppermute | solution.py:169
  83.2 24.9 %collective-permute-start.1 = (bf16[1024,256]{1,0:T(8,128)(2,1)}, bf16[1024,256]{1,0:T(8,128)(2,1)S(1)}, u32[]{:S(2)}, u32[]{:S(2)}) collective-permute-start(bf16[1024,256]{1,0:T(8,128)(2,1)} %collective-permute-done), channel_id=1, source_target_pairs={{0,2},{2,0},{4,6},{6,4},{8,10},{10,8},{12,14},{14,12},{16,18},{18,... | collective-permute-start | bytes 1572872 | tf_op jit(solution)/shard_map/ppermute | solution.py:170
  84.4 110.3 %collective-permute-start.13 = (bf16[1024,1024]{1,0:T(8,128)(2,1)S(1)}, bf16[1024,1024]{1,0:T(8,128)(2,1)}, u32[]{:S(2)}, u32[]{:S(2)}) collective-permute-start(bf16[1024,1024]{1,0:T(8,128)(2,1)S(1)} %constant_dynamic-slice_fusion), channel_id=1, source_target_pairs={{0,1},{1,0},{2,3},{3,2},{4,5},{5,4},{6,7},{7,6},{8,9},{9,8},{10,11... | collective-permute-start | bytes 6291464 | tf_op jit(solution)/shard_map/ppermute | solution.py:169
  96.0 17.4 %collective-permute-start.6 = (bf16[1024,256]{1,0:T(8,128)(2,1)}, bf16[1024,256]{1,0:T(8,128)(2,1)S(1)}, u32[]{:S(2)}, u32[]{:S(2)}) collective-permute-start(bf16[1024,256]{1,0:T(8,128)(2,1)} %collective-permute-done.5), channel_id=1, source_target_pairs={{0,2},{2,0},{4,6},{6,4},{8,10},{10,8},{12,14},{14,12},{16,18},{18,... | collective-permute-start | bytes 1572872 | tf_op jit(solution)/shard_map/ppermute | solution.py:170
  107.2 3.8 collective-permute-start.4
  108.1 27.5 %collective-permute-start.9 = (bf16[256,1024]{1,0:T(8,128)(2,1)S(1)}, bf16[256,1024]{1,0:T(8,128)(2,1)S(1)}, u32[]{:S(2)}, u32[]{:S(2)}) collective-permute-start(bf16[256,1024]{1,0:T(8,128)(2,1)S(1)} %collective-permute-done.8), channel_id=1, source_target_pairs={{0,2},{2,0},{4,6},{6,4},{8,10},{10,8},{12,14},{14,12},{16,18},{18,... | collective-permute-start | bytes 1572872 | tf_op jit(solution)/shard_map/ppermute | solution.py:170
  115.9 19.6 %copy-start.23 = (bf16[2048,512]{1,0:T(8,128)(2,1)}, bf16[2048,512]{1,0:T(8,128)(2,1)S(1)}, u32[]{:S(2)}) copy-start(bf16[2048,512]{1,0:T(8,128)(2,1)S(1)} %fusion.17.value_ref) | copy-start | bytes 6291460
  115.9 20.6 %copy-start.41 = (bf16[2048,1024]{0,1:T(8,128)(2,1)S(1)}, bf16[2048,1024]{0,1:T(8,128)(2,1)}, u32[]{:S(2)}) copy-start(bf16[2048,1024]{0,1:T(8,128)(2,1)} %copy.35) | copy-start | bytes 12582916
  142.2 70.9 %copy-start.77 = (f32[2048]{0:T(1024)}, f32[2048]{0:T(1024)S(1)}, u32[]{:S(2)}) copy-start(f32[2048]{0:T(1024)S(1)} %broadcast_multiply_fusion.5) | copy-start | bytes 24580
  145.6 67.5 %copy-start.84 = (f32[2048]{0:T(1024)}, f32[2048]{0:T(1024)S(1)}, u32[]{:S(2)}) copy-start(f32[2048]{0:T(1024)S(1)} %add_rsqrt_fusion.1) | copy-start | bytes 24580
  147.8 49.0 %copy-start.42 = (bf16[2048,1024]{0,1:T(8,128)(2,1)}, bf16[2048,1024]{0,1:T(8,128)(2,1)S(1)}, u32[]{:S(2)}) copy-start(bf16[2048,1024]{0,1:T(8,128)(2,1)S(1)} %fusion.7) | copy-start | bytes 12582916
  161.7 34.9 %collective-permute-start.11 = (bf16[1024,1024]{1,0:T(8,128)(2,1)S(1)}, bf16[1024,1024]{1,0:T(8,128)(2,1)S(1)}, u32[]{:S(2)}, u32[]{:S(2)}) collective-permute-start(bf16[1024,1024]{1,0:T(8,128)(2,1)S(1)} %collective-permute-done.10), channel_id=1, source_target_pairs={{0,2},{2,0},{4,6},{6,4},{8,10},{10,8},{12,14},{14,12},{16,18},{18,... | collective-permute-start | bytes 6291464 | tf_op jit(solution)/shard_map/ppermute | solution.py:170
  194.6 16.3 %collective-permute-start.14 = (bf16[1024,1024]{1,0:T(8,128)(2,1)}, bf16[1024,1024]{1,0:T(8,128)(2,1)S(1)}, u32[]{:S(2)}, u32[]{:S(2)}) collective-permute-start(bf16[1024,1024]{1,0:T(8,128)(2,1)} %collective-permute-done.13), channel_id=1, source_target_pairs={{0,2},{2,0},{4,6},{6,4},{8,10},{10,8},{12,14},{14,12},{16,18},{18,... | collective-permute-start | bytes 6291464 | tf_op jit(solution)/shard_map/ppermute | solution.py:170
  248.1 47.6 %copy-start.44 = (bf16[2048,1024]{0,1:T(8,128)(2,1)}, bf16[2048,1024]{0,1:T(8,128)(2,1)S(1)}, u32[]{:S(2)}) copy-start(bf16[2048,1024]{0,1:T(8,128)(2,1)S(1)} %fusion.50) | copy-start | bytes 12582916
  258.9 21.8 %copy-start.43 = (bf16[2048,1024]{0,1:T(8,128)(2,1)S(1)}, bf16[2048,1024]{0,1:T(8,128)(2,1)}, u32[]{:S(2)}) copy-start(bf16[2048,1024]{0,1:T(8,128)(2,1)} %copy-done.42) | copy-start | bytes 12582916
  372.5 17.4 %collective-permute-start.15 = (bf16[1024,1024]{1,0:T(8,128)(2,1)}, bf16[1024,1024]{1,0:T(8,128)(2,1)S(1)}, u32[]{:S(2)}, u32[]{:S(2)}) collective-permute-start(bf16[1024,1024]{1,0:T(8,128)(2,1)} %split.99), channel_id=1, source_target_pairs={{0,2},{2,0},{4,6},{6,4},{8,10},{10,8},{12,14},{14,12},{16,18},{18,... | collective-permute-start | bytes 6291464 | tf_op jit(solution)/shard_map/ppermute | solution.py:179
  374.5 15.4 %collective-permute-start.16 = (bf16[1024,1024]{1,0:T(8,128)(2,1)}, bf16[1024,1024]{1,0:T(8,128)(2,1)}, u32[]{:S(2)}, u32[]{:S(2)}) collective-permute-start(bf16[1024,1024]{1,0:T(8,128)(2,1)} %split.100), channel_id=1, source_target_pairs={{0,2},{2,0},{4,6},{6,4},{8,10},{10,8},{12,14},{14,12},{16,18},{18,... | collective-permute-start | bytes 6291464 | tf_op jit(solution)/shard_map/ppermute | solution.py:179
  417.7 44.8 %copy-start.38 = (bf16[2048,1024]{1,0:T(8,128)(2,1)S(1)}, bf16[2048,1024]{1,0:T(8,128)(2,1)}, u32[]{:S(2)}) copy-start(bf16[2048,1024]{1,0:T(8,128)(2,1)} %param.18) | copy-start | bytes 12582916
  475.7 48.7 %collective-permute-start.18 = (bf16[1024,1024]{1,0:T(8,128)(2,1)}, bf16[1024,1024]{1,0:T(8,128)(2,1)}, u32[]{:S(2)}, u32[]{:S(2)}) collective-permute-start(bf16[1024,1024]{1,0:T(8,128)(2,1)} %add_convert_fusion.2), channel_id=1, source_target_pairs={{0,1},{1,0},{2,3},{3,2},{4,5},{5,4},{6,7},{7,6},{8,9},{9,8},{10,11... | collective-permute-start | bytes 6291464 | tf_op jit(solution)/shard_map/ppermute | solution.py:184
  478.3 90.6 %collective-permute-start.17 = (bf16[1024,1024]{1,0:T(8,128)(2,1)}, bf16[1024,1024]{1,0:T(8,128)(2,1)}, u32[]{:S(2)}, u32[]{:S(2)}) collective-permute-start(bf16[1024,1024]{1,0:T(8,128)(2,1)} %add_convert_fusion.3), channel_id=1, source_target_pairs={{0,1},{1,0},{2,3},{3,2},{4,5},{5,4},{6,7},{7,6},{8,9},{9,8},{10,11... | collective-permute-start | bytes 6291464 | tf_op jit(solution)/shard_map/ppermute | solution.py:184
  501.5 67.5 %slice-start.4 = ((s8[8388608]{0:T(1024)(128)(4,1)}), s8[4194304]{0:T(1024)(128)(4,1)S(1)}, s32[]{:S(2)}) async-start(s8[8388608]{0:T(1024)(128)(4,1)} %bitcast.108), calls=%async_computation.6 | async-start | bytes 8388608
  501.5 67.5 %slice-start.6 = ((s8[8388608]{0:T(1024)(128)(4,1)}), s8[4194304]{0:T(1024)(128)(4,1)S(1)}, s32[]{:S(2)}) async-start(s8[8388608]{0:T(1024)(128)(4,1)} %bitcast.110), calls=%async_computation.8 | async-start | bytes 8388608
  504.9 64.1 %slice-start.5 = ((s8[8388608]{0:T(1024)(128)(4,1)}), s8[4194304]{0:T(1024)(128)(4,1)S(1)}, s32[]{:S(2)}) async-start(s8[8388608]{0:T(1024)(128)(4,1)} %bitcast.108), calls=%async_computation.7 | async-start | bytes 8388608
  504.9 64.1 %slice-start.7 = ((s8[8388608]{0:T(1024)(128)(4,1)}), s8[4194304]{0:T(1024)(128)(4,1)S(1)}, s32[]{:S(2)}) async-start(s8[8388608]{0:T(1024)(128)(4,1)} %bitcast.110), calls=%async_computation.9 | async-start | bytes 8388608
  586.8 48.5 %copy-start.55 = (bf16[512,1024]{1,0:T(8,128)(2,1)S(1)}, bf16[512,1024]{1,0:T(8,128)(2,1)}, u32[]{:S(2)}) copy-start(bf16[512,1024]{1,0:T(8,128)(2,1)} %convolution_convert_fusion.9) | copy-start | bytes 3145732
  586.8 49.3 %copy-start.53 = (bf16[1024,512]{0,1:T(8,128)(2,1)S(1)}, bf16[1024,512]{0,1:T(8,128)(2,1)}, u32[]{:S(2)}) copy-start(bf16[1024,512]{0,1:T(8,128)(2,1)} %fusion.19) | copy-start | bytes 3145732
  586.8 50.6 %copy-start.56 = (bf16[1024,512]{0,1:T(8,128)(2,1)S(1)}, bf16[1024,512]{0,1:T(8,128)(2,1)}, u32[]{:S(2)}) copy-start(bf16[1024,512]{0,1:T(8,128)(2,1)} %fusion.20) | copy-start | bytes 3145732
  586.8 51.4 %copy-start.58 = (bf16[1024,512]{0,1:T(8,128)(2,1)S(1)}, bf16[1024,512]{0,1:T(8,128)(2,1)}, u32[]{:S(2)}) copy-start(bf16[1024,512]{0,1:T(8,128)(2,1)} %fusion.21) | copy-start | bytes 3145732
  636.1 10.9 %collective-permute-start.19 = (bf16[256,1024]{1,0:T(8,128)(2,1)}, bf16[256,1024]{1,0:T(8,128)(2,1)}, u32[]{:S(2)}, u32[]{:S(2)}) collective-permute-start(bf16[256,1024]{1,0:T(8,128)(2,1)} %split.107), channel_id=1, source_target_pairs={{0,2},{2,0},{4,6},{6,4},{8,10},{10,8},{12,14},{14,12},{16,18},{18,... | collective-permute-start | bytes 1572872 | tf_op jit(solution)/shard_map/ppermute | solution.py:179
  636.9 10.1 %collective-permute-start.20 = (bf16[1024,256]{0,1:T(8,128)(2,1)}, bf16[1024,256]{0,1:T(8,128)(2,1)}, u32[]{:S(2)}, u32[]{:S(2)}) collective-permute-start(bf16[1024,256]{0,1:T(8,128)(2,1)} %split.108), channel_id=1, source_target_pairs={{0,2},{2,0},{4,6},{6,4},{8,10},{10,8},{12,14},{14,12},{16,18},{18,... | collective-permute-start | bytes 1572872 | tf_op jit(solution)/shard_map/ppermute | solution.py:179
  638.2 8.8 collective-permute-start.21
  639.1 7.9 collective-permute-start.22
  640.0 287.7 %all-reduce.5.cloned.1.call-start = ((), (), s32[]{:S(2)}) async-start(), calls=%async_computation | async-start | bytes 8388608 | tf_op jit(solution)/shard_map/psum | solution.py:385
  658.5 80.0 %collective-permute-start.26 = (bf16[1024,256]{0,1:T(8,128)(2,1)}, bf16[1024,256]{0,1:T(8,128)(2,1)}, u32[]{:S(2)}, u32[]{:S(2)}) collective-permute-start(bf16[1024,256]{0,1:T(8,128)(2,1)} %add_convert_fusion.8), channel_id=1, source_target_pairs={{0,1},{1,0},{2,3},{3,2},{4,5},{5,4},{6,7},{7,6},{8,9},{9,8},{10,11... | collective-permute-start | bytes 1572872 | tf_op jit(solution)/shard_map/ppermute | solution.py:184
  661.0 80.6 %collective-permute-start.25 = (bf16[1024,256]{0,1:T(8,128)(2,1)}, bf16[1024,256]{0,1:T(8,128)(2,1)}, u32[]{:S(2)}, u32[]{:S(2)}) collective-permute-start(bf16[1024,256]{0,1:T(8,128)(2,1)} %add_convert_fusion.9), channel_id=1, source_target_pairs={{0,1},{1,0},{2,3},{3,2},{4,5},{5,4},{6,7},{7,6},{8,9},{9,8},{10,11... | collective-permute-start | bytes 1572872 | tf_op jit(solution)/shard_map/ppermute | solution.py:184
  683.8 60.3 %collective-permute-start.24 = (bf16[1024,256]{0,1:T(8,128)(2,1)}, bf16[1024,256]{0,1:T(8,128)(2,1)}, u32[]{:S(2)}, u32[]{:S(2)}) collective-permute-start(bf16[1024,256]{0,1:T(8,128)(2,1)} %add_convert_fusion.10), channel_id=1, source_target_pairs={{0,1},{1,0},{2,3},{3,2},{4,5},{5,4},{6,7},{7,6},{8,9},{9,8},{10,11... | collective-permute-start | bytes 1572872 | tf_op jit(solution)/shard_map/ppermute | solution.py:184
  735.0 13.0 %collective-permute-start.23 = (bf16[256,1024]{1,0:T(8,128)(2,1)S(1)}, bf16[256,1024]{1,0:T(8,128)(2,1)S(1)}, u32[]{:S(2)}, u32[]{:S(2)}) collective-permute-start(bf16[256,1024]{1,0:T(8,128)(2,1)S(1)} %add_convert_fusion.11), channel_id=1, source_target_pairs={{0,1},{1,0},{2,3},{3,2},{4,5},{5,4},{6,7},{7,6},{8,9},{9,8},{10,11... | collective-permute-start | bytes 1572872 | tf_op jit(solution)/shard_map/ppermute | solution.py:184
  (92 other events, 661.6 us)
Sparse Core Ops, SparseCore 0:
  640.1 170.5 all-reduce.6
  815.9 111.6 all-reduce.4
